TPU v7x, 32 devices: a whole 2x2x4 slice. The times are simulated.
32 devices in a mesh: dom: 8 (over y, x, core), band: 4 (over z).
Axes of the slice: x: 2, y: 2, z: 4, core: 2. Of those that a mesh axis runs over, the one named last changes fastest.
Arguments:
- states: bfloat16 [256, 98304], P('band', 'dom'), may hold values from -640 to 640
- cell_kinetic: bfloat16 [512, 512], replicated, may hold values from -0.3 to 0.3, as said below
- cell_scale: float32 [256], P('dom'), may hold values from 0.5 to 2
- cell_potential: float32 [256, 512], P('dom'), may hold values from -0.3 to 0.3
- connectivity: int32 [256, 512], P('dom'), may hold values from 0 to 12287, as said below
- shared_nodes: int32 [8, 2, 1024], P('dom'), may hold values from 0 to 12287, as said below
- cell_counts: int32 [8], P('dom'), may hold values from 4 to 32, as said below
Outputs:
- rotated: bfloat16 [256, 98304], P('band', 'dom')
Inputs may be any that keep to these rules, and one draw needn't show every extreme that they name: cell_kinetic is symmetric. `connectivity`: row c of a domain (local cell number c) names each of the 512 nodes c * 3 * 128 to c * 3 * 128 + 511, counted round modulo 12288, exactly once. `shared_nodes`: the two rows of a domain name 2048 distinct nodes; position p of domain d's row 1 and of domain d+1's row 0 are the same physical node. `cell_counts`: in every draw some domain has all 32 cells live.
All inputs are finite; a program needn't handle non-finite values.
Results may differ from a plain program's by a relative error of at most 0.008.
Values may be sent and summed in bfloat16 or wider, within the bound.
A program may use at most 128 MiB of HBM per device.

v0:
```python
import math

import jax
import jax.numpy as jnp
from jax import lax
from jax.sharding import PartitionSpec as P

CHEB = 4
NS_ITERS = 5


def with_halo(x, sides, width):
    for axis, dim in sides:
        size, length = (lax.axis_size(axis), x.shape[dim])
        up = [(i, (i + 1) % size) for i in range(size - 1)]
        down = [(j, i) for i, j in up]
        last = lax.slice_in_dim(x, length - width, length, axis=dim)
        first = lax.slice_in_dim(x, 0, width, axis=dim)
        before = lax.ppermute(last, axis, up)
        after = lax.ppermute(first, axis, down)
        x = jnp.concatenate([before, x, after], axis=dim)
    return x


def window_operators(connectivity, cell_kinetic, cell_potential, node_total):
    cell_total = connectivity.shape[0]
    width = connectivity.shape[1]
    quarter = width // 4
    starts = jnp.arange(cell_total, dtype=jnp.int32) * (3 * quarter)
    slots = (connectivity - starts[:, None]) % node_total
    onehot = (slots[:, :, None] == jnp.arange(width, dtype=jnp.int32)[None, None, :]).astype(
        jnp.bfloat16
    )
    kinetic_cols = jnp.einsum(
        "ij,cia->cja", cell_kinetic, onehot, preferred_element_type=jnp.float32
    ).astype(jnp.bfloat16)
    window_ops = jnp.einsum(
        "cjb,cja->cba", onehot, kinetic_cols, preferred_element_type=jnp.float32
    ).astype(jnp.bfloat16)
    window_pot = jnp.einsum(
        "ci,cia->ca", cell_potential, onehot.astype(jnp.float32), precision=lax.Precision.HIGHEST
    )
    return (window_ops, window_pot)


def window_terms(windows, window_ops, scales, window_pot, alive_mask):
    product = jnp.einsum("scb,cba->sca", windows, window_ops, preferred_element_type=jnp.float32)
    return (
        product * scales[None, :, None] + window_pot[None] * windows.astype(jnp.float32)
    ) * alive_mask[None, :, None]


def local_apply(vector, window_ops, window_pot, scales, live_count):
    state_rows, node_total = vector.shape
    cell_total, width = window_pot.shape
    quarter = width // 4
    blocked = vector.reshape(state_rows, cell_total, 3, quarter)
    following = jnp.roll(blocked[:, :, 0], -1, axis=1)
    windows = jnp.concatenate([blocked, following[:, :, None]], axis=2).reshape(
        state_rows, cell_total, width
    )
    block_size = math.gcd(cell_total, 16)

    def visit_block(block_index, collected):
        first_cell = block_index * block_size
        window_block = lax.dynamic_slice_in_dim(windows, first_cell, block_size, 1)
        ops_block = lax.dynamic_slice_in_dim(window_ops, first_cell, block_size, 0)
        scale_block = lax.dynamic_slice_in_dim(scales, first_cell, block_size, 0)
        pot_block = lax.dynamic_slice_in_dim(window_pot, first_cell, block_size, 0)
        alive_mask = (first_cell + jnp.arange(block_size) < live_count).astype(jnp.float32)
        block_terms = window_terms(window_block, ops_block, scale_block, pot_block, alive_mask)
        return lax.dynamic_update_slice_in_dim(collected, block_terms, first_cell, 1)

    blocks = (live_count + block_size - 1) // block_size
    terms = lax.fori_loop(
        0, blocks, visit_block, jnp.zeros((state_rows, cell_total, width), jnp.float32)
    )
    split_terms = terms.reshape(state_rows, cell_total, 4, quarter)
    folded = split_terms[:, :, :3]
    folded = folded.at[:, :, 0].add(jnp.roll(split_terms[:, :, 3], 1, axis=1))
    return folded.reshape(state_rows, node_total)


def newton(gram_matrix):
    identity = jnp.eye(gram_matrix.shape[0], dtype=jnp.float32)
    frobenius = jnp.sqrt(jnp.sum(gram_matrix * gram_matrix))
    scaled = gram_matrix / frobenius
    inverse_root = identity
    for repeat in range(NS_ITERS):
        factor = 1.5 * identity - 0.5 * jnp.dot(
            inverse_root, scaled, precision=lax.Precision.HIGHEST
        )
        scaled = jnp.dot(scaled, factor, precision=lax.Precision.HIGHEST)
        inverse_root = jnp.dot(factor, inverse_root, precision=lax.Precision.HIGHEST)
    return inverse_root.astype(jnp.bfloat16)


def body(states, cell_kinetic, cell_scale, cell_potential, connectivity, shared_nodes, cell_counts):
    left_face = shared_nodes[0, 0]
    right_face = shared_nodes[0, 1]
    live_count = cell_counts[0]
    domain = lax.axis_index("dom")
    domains = lax.axis_size("dom")
    node_total = states.shape[1]
    has_left = (domain > 0).astype(jnp.float32)
    has_right = (domain < domains - 1).astype(jnp.float32)
    multiplicity = (
        jnp.ones((node_total,), jnp.float32)
        .at[left_face]
        .add(has_left)
        .at[right_face]
        .add(has_right)
    )
    node_weight = (1.0 / multiplicity).astype(jnp.bfloat16)
    window_ops, window_pot = window_operators(
        connectivity, cell_kinetic, cell_potential, node_total
    )

    def apply_field(vector):
        local_sum = local_apply(vector, window_ops, window_pot, cell_scale, live_count)
        face_values = jnp.stack([local_sum[:, left_face], local_sum[:, right_face]], axis=1)
        padded = with_halo(face_values, (("dom", 1),), 1)
        return local_sum.at[:, left_face].add(padded[:, 0]).at[:, right_face].add(padded[:, 3])

    previous = states
    current = apply_field(states).astype(jnp.bfloat16)
    for repeat in range(CHEB - 1):
        following = (2.0 * apply_field(current) - previous.astype(jnp.float32)).astype(jnp.bfloat16)
        previous = current
        current = following
    row_shard = lax.all_to_all(current, "band", split_axis=1, concat_axis=0, tiled=True)
    piece_nodes = row_shard.shape[1]
    weight_rows = lax.dynamic_slice_in_dim(
        node_weight, lax.axis_index("band") * piece_nodes, piece_nodes, 0
    )
    weighted = row_shard * weight_rows[None]
    partial_gram = lax.dot_general(
        weighted, row_shard, (((1,), (1,)), ((), ())), preferred_element_type=jnp.float32
    )
    gram_matrix = lax.psum(partial_gram, ("dom", "band"))
    mixing = newton(gram_matrix)
    rotated = lax.dot_general(
        mixing, row_shard, (((0,), (0,)), ((), ())), preferred_element_type=jnp.float32
    ).astype(jnp.bfloat16)
    return lax.all_to_all(rotated, "band", split_axis=0, concat_axis=1, tiled=True)


def solution(mesh):
    in_specs = (
        P("band", "dom"),
        P(),
        P("dom"),
        P("dom", None),
        P("dom", None),
        P("dom", None, None),
        P("dom"),
    )
    out_specs = P("band", "dom")
    return jax.shard_map(body, mesh=mesh, in_specs=in_specs, out_specs=out_specs, check_vma=False)
```

profile of v0, /device:TPU:9, one launch (start us, length us, event | category | flops | bytes accessed | tf_op | source)
XLA Modules:
  0.0 688.5 jit_solution(8151074056516918234)
XLA Ops:
  12.4 8.4 %iota_compare_fusion.21 = pred[32,512,512]{1,2,0:T(32,128)(4,1)} fusion(s32[32,512]{1,0:T(8,128)S(1)} %add_select_fusion), kind=kLoop, calls=%fused_computation.55.clone.1.clone.clone.clone.2 | loop fusion | flops 8388608 | bytes 8454144 | tf_op jit(solution)/shard_map/cjb,cja->cba/dot_general | solution.py:37
  28.3 14.8 %fusion.32 = f32[32,1,512]{2,1,0:T(1,128)S(1)} fusion(s32[32,512]{1,0:T(8,128)S(1)} %add_select_fusion, f32[32,512,1]{1,0,2:T(8,128)S(1)} %bitcast.288), kind=kOutput, calls=%fused_computation.56 | convolution fusion | flops 109051904 | bytes 196608 | tf_op jit(solution)/shard_map/ci,cia->ca/dot_general | solution.py:40
  43.1 21.8 %fusion.39 = bf16[32,512,512]{2,1,0:T(8,128)(2,1)} fusion(s32[32,512]{1,0:T(8,128)S(1)} %add_select_fusion, bf16[512,512]{1,0:T(8,128)(2,1)S(1)} %copy-done, pred[32,512,512]{1,2,0:T(32,128)(4,1)} %iota_compare_fusion.21), kind=kOutput, calls=%fused_computation.62 | convolution fusion | flops 17205035008 | bytes 25755648 | tf_op jit(solution)/shard_map/cjb,cja->cba/dot_general | solution.py:37
  67.5 8.4 %while.44 = (s32[]{:T(128)}, f32[64,32,512]{2,0,1:T(8,128)}, s32[]{:T(128)}, bf16[32,512,512]{2,1,0:T(8,128)(2,1)}, bf16[64,32,512]{2,1,0:T(8,128)(2,1)S(1)}, /*...) while((s32[]{:T(128)}, f32[64,32,512]{2,0,1:T(8,128)}, ...), condition=%wide.region_1.0_spmd, body=%wide.region_0.0_spmd.sunk | while | flops 539492416 | bytes 14780791 | solution.py:75
  68.3 7.6 %fusion.139 = f32[64,32,512]{2,0,1:T(8,128)} fusion(f32[64,32,512]{2,0,1:T(8,128)} %get-tuple-element.532, s32[]{:T(128)S(6)} %select_n.93, bf16[32,512,512]{2,1,0:T(8,128)(2,1)} %get-tuple-element.546, bf16[64,16,512]{2,1,0:T(8,128)(2,1)S(1)} %constant_dynamic-slice_fusion.10, f32[16]{0:T(128)S(1)} %compare_convert_fusion.8, ...), kind=kOutput, calls=%fused_computation.22.clone.1 | convolution fusion | flops 539492352 | bytes 12617728 | tf_op jit(solution)/shard_map/while/body/scb,cba->sca/dot_general | solution.py:47
  81.1 7.0 %fusion.82 = (f32[64,32,1,128]{3,2,0,1:T(1,128)}, f32[64,32,1,128]{3,2,0,1:T(1,128)}) fusion(f32[64,32,4,128]{3,2,0,1:T(4,128)} %reshape.296), kind=kLoop, calls=%fused_computation.141 | loop fusion | bytes 4194304 | tf_op jit(solution)/shard_map/slice | solution.py:80
  94.7 6.9 copy.83
  104.9 5.6 gather_fusion
  114.2 6.0 gather_fusion.1
  120.1 8.7 %collective-permute-start.1 = (f32[64,1,1024]{0,2,1:T(8,128)S(1)}, f32[64,1,1024]{0,2,1:T(8,128)S(1)}, u32[]{:S(2)}, u32[]{:S(2)}) collective-permute-start(f32[64,1,1024]{0,2,1:T(8,128)S(1)} %bitcast.273), channel_id=1, source_target_pairs={{4,0},{8,4},{12,8},{16,12},{20,16},{24,20},{28,24},{5,1},{9,5},{13... | collective-permute-start | bytes 786440 | tf_op jit(solution)/shard_map/ppermute | solution.py:20
  128.8 10.9 %scatter_custom_fusion = f32[64,12288]{0,1:T(8,128)} fusion(f32[64,12288]{0,1:T(8,128)} %bitcast.229, s32[1024]{0:T(1024)S(1)} %bitcast.283, f32[64,1,1024]{0,2,1:T(8,128)S(1)} %collective-permute-done), kind=kCustom, calls=%fused_computation.117 | custom fusion | flops 65536 | bytes 3670016 | tf_op jit(solution)/shard_map/scatter-add | solution.py:123
  139.7 10.9 %scatter_custom_fusion.1 = f32[64,12288]{0,1:T(8,128)} fusion(f32[64,12288]{0,1:T(8,128)} %scatter_custom_fusion, s32[1024]{0:T(1024)S(1)} %bitcast.277, f32[64,1,1024]{0,2,1:T(8,128)S(1)} %collective-permute-done.1), kind=kCustom, calls=%fused_computation.115 | custom fusion | flops 65536 | bytes 3670016 | tf_op jit(solution)/shard_map/scatter-add | solution.py:123
  162.8 6.9 %while.45 = (s32[]{:T(128)}, f32[64,32,512]{2,0,1:T(8,128)}, s32[]{:T(128)}, bf16[32,512,512]{2,1,0:T(8,128)(2,1)}, bf16[64,32,512]{2,0,1:T(8,128)(2,1)S(1)}, /*...) while((s32[]{:T(128)}, f32[64,32,512]{2,0,1:T(8,128)}, ...), condition=%wide.region_5.6_spmd, body=%wide.region_4.5_spmd.sunk | while | flops 539492416 | bytes 12683251 | solution.py:75
  163.5 6.2 fusion.142
  169.7 5.3 reshape.301
  175.0 7.0 %fusion.81 = (f32[64,32,1,128]{3,2,0,1:T(1,128)}, f32[64,32,1,128]{3,2,0,1:T(1,128)}) fusion(f32[64,32,4,128]{3,2,0,1:T(4,128)} %reshape.301), kind=kLoop, calls=%fused_computation.140 | loop fusion | bytes 4194304 | tf_op jit(solution)/shard_map/slice | solution.py:80
  186.0 6.9 %copy.87 = f32[64,32,3,128]{0,3,2,1:T(8,128)} copy(f32[64,32,3,128]{3,2,0,1:T(4,128)} %bitcast.242) | data formatting | bytes 6291456
  198.6 6.9 %gather_fusion.2 = f32[1024,64]{1,0:T(8,128)} fusion(f32[64,12288]{0,1:T(8,128)} %bitcast.230, s32[1024]{0:T(1024)S(1)} %broadcast_clamp_fusion.1), kind=kCustom, calls=%fused_computation.2 | custom fusion | bytes 528384 | tf_op jit(solution)/shard_map/gather | solution.py:121
  205.6 5.6 gather_fusion.3
  213.1 7.6 %collective-permute-start.3 = (f32[64,1,1024]{0,2,1:T(8,128)S(1)}, f32[64,1,1024]{0,2,1:T(8,128)S(1)}, u32[]{:S(2)}, u32[]{:S(2)}) collective-permute-start(f32[64,1,1024]{0,2,1:T(8,128)S(1)} %bitcast.269), channel_id=1, source_target_pairs={{4,0},{8,4},{12,8},{16,12},{20,16},{24,20},{28,24},{5,1},{9,5},{13... | collective-permute-start | bytes 786440 | tf_op jit(solution)/shard_map/ppermute | solution.py:20
  223.7 10.9 %scatter_custom_fusion.2 = f32[64,12288]{0,1:T(8,128)} fusion(f32[64,12288]{0,1:T(8,128)} %bitcast.232, s32[1024]{0:T(1024)S(1)} %bitcast.284, f32[64,1,1024]{0,2,1:T(8,128)S(1)} %collective-permute-done.2), kind=kCustom, calls=%fused_computation.113 | custom fusion | flops 65536 | bytes 3670016 | tf_op jit(solution)/shard_map/scatter-add | solution.py:123
  234.6 10.9 %scatter_custom_fusion.3 = f32[64,12288]{0,1:T(8,128)} fusion(f32[64,12288]{0,1:T(8,128)} %scatter_custom_fusion.2, s32[1024]{0:T(1024)S(1)} %bitcast.278, f32[64,1,1024]{0,2,1:T(8,128)S(1)} %collective-permute-done.3), kind=kCustom, calls=%fused_computation.111 | custom fusion | flops 65536 | bytes 3670016 | tf_op jit(solution)/shard_map/scatter-add | solution.py:123
  258.8 7.0 %while.46 = (s32[]{:T(128)}, f32[64,32,512]{2,0,1:T(8,128)}, s32[]{:T(128)}, bf16[32,512,512]{2,1,0:T(8,128)(2,1)}, bf16[64,32,512]{2,0,1:T(8,128)(2,1)S(1)}, /*...) while((s32[]{:T(128)}, f32[64,32,512]{2,0,1:T(8,128)}, ...), condition=%wide.region_9.10_spmd, body=%wide.region_8.9_spmd.sunk | while | flops 539492416 | bytes 12683251 | solution.py:75
  259.6 6.2 fusion.145
  271.1 7.0 %fusion.80 = (f32[64,32,1,128]{3,2,0,1:T(1,128)}, f32[64,32,1,128]{3,2,0,1:T(1,128)}) fusion(f32[64,32,4,128]{3,2,0,1:T(4,128)} %reshape.306), kind=kLoop, calls=%fused_computation.139 | loop fusion | bytes 4194304 | tf_op jit(solution)/shard_map/slice | solution.py:80
  282.1 6.9 %copy.91 = f32[64,32,3,128]{0,3,2,1:T(8,128)} copy(f32[64,32,3,128]{3,2,0,1:T(4,128)} %bitcast.243) | data formatting | bytes 6291456
  294.8 5.6 gather_fusion.4
  300.4 5.6 gather_fusion.5
  307.9 7.8 %collective-permute-start.5 = (f32[64,1,1024]{0,2,1:T(8,128)S(1)}, f32[64,1,1024]{0,2,1:T(8,128)S(1)}, u32[]{:S(2)}, u32[]{:S(2)}) collective-permute-start(f32[64,1,1024]{0,2,1:T(8,128)S(1)} %bitcast.270), channel_id=1, source_target_pairs={{4,0},{8,4},{12,8},{16,12},{20,16},{24,20},{28,24},{5,1},{9,5},{13... | collective-permute-start | bytes 786440 | tf_op jit(solution)/shard_map/ppermute | solution.py:20
  315.7 10.9 %scatter_custom_fusion.4 = f32[64,12288]{0,1:T(8,128)} fusion(f32[64,12288]{0,1:T(8,128)} %bitcast.235, s32[1024]{0:T(1024)S(1)} %bitcast.285, f32[64,1,1024]{0,2,1:T(8,128)S(1)} %collective-permute-done.4), kind=kCustom, calls=%fused_computation.109 | custom fusion | flops 65536 | bytes 3670016 | tf_op jit(solution)/shard_map/scatter-add | solution.py:123
  326.6 10.9 %scatter_custom_fusion.5 = f32[64,12288]{0,1:T(8,128)} fusion(f32[64,12288]{0,1:T(8,128)} %scatter_custom_fusion.4, s32[1024]{0:T(1024)S(1)} %bitcast.279, f32[64,1,1024]{0,2,1:T(8,128)S(1)} %collective-permute-done.5), kind=kCustom, calls=%fused_computation.107 | custom fusion | flops 65536 | bytes 3670016 | tf_op jit(solution)/shard_map/scatter-add | solution.py:123
  351.7 6.9 %while.47 = (s32[]{:T(128)}, f32[64,32,512]{2,0,1:T(8,128)}, s32[]{:T(128)}, bf16[32,512,512]{2,1,0:T(8,128)(2,1)}, bf16[64,32,512]{2,0,1:T(8,128)(2,1)S(1)}, /*...) while((s32[]{:T(128)}, f32[64,32,512]{2,0,1:T(8,128)}, ...), condition=%wide.region_13.14_spmd, body=%wide.region_12.13_spmd.sunk | while | flops 539492416 | bytes 12683251 | solution.py:75
  352.4 6.2 fusion.148
  358.6 5.3 reshape.311
  363.9 7.0 %fusion.79 = (f32[64,32,1,128]{3,2,0,1:T(1,128)}, f32[64,32,1,128]{3,2,0,1:T(1,128)}) fusion(f32[64,32,4,128]{3,2,0,1:T(4,128)} %reshape.311), kind=kLoop, calls=%fused_computation.138 | loop fusion | bytes 4194304 | tf_op jit(solution)/shard_map/slice | solution.py:80
  374.9 6.9 %copy.95 = f32[64,32,3,128]{0,3,2,1:T(8,128)} copy(f32[64,32,3,128]{3,2,0,1:T(4,128)} %bitcast.244) | data formatting | bytes 6291456
  387.5 5.6 gather_fusion.6
  393.1 5.6 gather_fusion.7
  401.4 7.2 %collective-permute-start.7 = (f32[64,1,1024]{0,2,1:T(8,128)S(1)}, f32[64,1,1024]{0,2,1:T(8,128)S(1)}, u32[]{:S(2)}, u32[]{:S(2)}) collective-permute-start(f32[64,1,1024]{0,2,1:T(8,128)S(1)} %bitcast.271), channel_id=1, source_target_pairs={{4,0},{8,4},{12,8},{16,12},{20,16},{24,20},{28,24},{5,1},{9,5},{13... | collective-permute-start | bytes 786440 | tf_op jit(solution)/shard_map/ppermute | solution.py:20
  408.6 10.9 %scatter_custom_fusion.6 = f32[64,12288]{0,1:T(8,128)} fusion(f32[64,12288]{0,1:T(8,128)} %bitcast.238, s32[1024]{0:T(1024)S(1)} %bitcast.286, f32[64,1,1024]{0,2,1:T(8,128)S(1)} %collective-permute-done.6), kind=kCustom, calls=%fused_computation.105 | custom fusion | flops 65536 | bytes 3670016 | tf_op jit(solution)/shard_map/scatter-add | solution.py:123
  419.5 9.5 %collective-permute-done.7 = f32[64,1,1024]{0,2,1:T(8,128)S(1)} collective-permute-done((f32[64,1,1024]{0,2,1:T(8,128)S(1)}, f32[64,1,1024]{0,2,1:T(8,128)S(1)}, u32[]{:S(2)}, u32[]{:S(2)}) %collective-permute-start.7) | collective-permute-done | bytes 262176 | tf_op jit(solution)/shard_map/ppermute | solution.py:20
  429.0 10.9 %scatter_custom_fusion.7 = f32[64,12288]{0,1:T(8,128)} fusion(f32[64,12288]{0,1:T(8,128)} %scatter_custom_fusion.6, s32[1024]{0:T(1024)S(1)} %bitcast.280, f32[64,1,1024]{0,2,1:T(8,128)S(1)} %collective-permute-done.7), kind=kCustom, calls=%fused_computation.103 | custom fusion | flops 65536 | bytes 3670016 | tf_op jit(solution)/shard_map/scatter-add | solution.py:123
  439.9 5.4 subtract_convert_fusion
  454.4 5.9 scatter_custom_fusion.8
  460.3 6.2 scatter_fusion
  466.6 12.9 %all-to-all-done = bf16[64,4,3072]{2,0,1:T(8,128)(2,1)S(1)} async-done(((bf16[64,4,3072]{2,0,1:T(8,128)(2,1)}), bf16[64,4,3072]{2,0,1:T(8,128)(2,1)S(1)}, u32[]{:S(2)}, u32[]{:S(2)}) %all-to-all-start) | async-done | bytes 1572896 | tf_op jit(solution)/shard_map/all_to_all | solution.py:131
  481.0 151.3 %all-reduce.2.cloned.1.call-done = f32[256,256]{1,0:T(8,128)} async-done(((f32[256,256]{1,0:T(8,128)}), f32[256,256]{1,0:T(8,128)}) %all-reduce.2.cloned.1.call-update) | async-done | bytes 262160 | tf_op jit(solution)/shard_map/psum | solution.py:140
  642.4 37.9 %all_to_all.38 = bf16[4,64,3072]{2,1,0:T(8,128)(2,1)S(1)} all-to-all(bf16[4,64,3072]{2,1,0:T(8,128)(2,1)S(1)} %bitcast.264), channel_id=1, replica_groups=mesh['dom'=8,'band'=4] {'band'}, dimensions={0} | all-to-all | bytes 3145728 | tf_op jit(solution)/shard_map/all_to_all | solution.py:145
  (129 shorter events, 141.4 us)
Async XLA Ops:
  6.5 36.6 %copy-start = (bf16[512,512]{1,0:T(8,128)(2,1)S(1)}, bf16[512,512]{1,0:T(8,128)(2,1)}, u32[]{:S(2)}) copy-start(bf16[512,512]{1,0:T(8,128)(2,1)} %param.24) | copy-start | bytes 1572868
  7.3 5.1 copy-start.4
  22.1 6.2 copy-start.6
  64.9 2.5 copy-start.7
  94.7 6.9 copy-start.5
  110.5 18.4 %collective-permute-start = (f32[64,1,1024]{0,2,1:T(8,128)S(1)}, f32[64,1,1024]{0,2,1:T(8,128)S(1)}, u32[]{:S(2)}, u32[]{:S(2)}) collective-permute-start(f32[64,1,1024]{0,2,1:T(8,128)S(1)} %bitcast.272), channel_id=1, source_target_pairs={{0,4},{4,8},{8,12},{12,16},{16,20},{20,24},{24,28},{1,5},{5,9},{9,... | collective-permute-start | bytes 786440 | tf_op jit(solution)/shard_map/ppermute | solution.py:19
  120.1 19.6 %collective-permute-start.1 = (f32[64,1,1024]{0,2,1:T(8,128)S(1)}, f32[64,1,1024]{0,2,1:T(8,128)S(1)}, u32[]{:S(2)}, u32[]{:S(2)}) collective-permute-start(f32[64,1,1024]{0,2,1:T(8,128)S(1)} %bitcast.273), channel_id=1, source_target_pairs={{4,0},{8,4},{12,8},{16,12},{20,16},{24,20},{28,24},{5,1},{9,5},{13... | collective-permute-start | bytes 786440 | tf_op jit(solution)/shard_map/ppermute | solution.py:20
  198.6 22.1 %copy-start.3 = (bf16[64,12288]{1,0:T(8,128)(2,1)S(1)}, bf16[64,12288]{1,0:T(8,128)(2,1)}, u32[]{:S(2)}) copy-start(bf16[64,12288]{1,0:T(8,128)(2,1)} %param.23) | copy-start | bytes 4718596
  211.2 12.5 %collective-permute-start.2 = (f32[64,1,1024]{0,2,1:T(8,128)}, f32[64,1,1024]{0,2,1:T(8,128)S(1)}, u32[]{:S(2)}, u32[]{:S(2)}) collective-permute-start(f32[64,1,1024]{0,2,1:T(8,128)} %bitcast.32), channel_id=1, source_target_pairs={{0,4},{4,8},{8,12},{12,16},{16,20},{20,24},{24,28},{1,5},{5,9},{9,... | collective-permute-start | bytes 786440 | tf_op jit(solution)/shard_map/ppermute | solution.py:19
  213.1 21.5 %collective-permute-start.3 = (f32[64,1,1024]{0,2,1:T(8,128)S(1)}, f32[64,1,1024]{0,2,1:T(8,128)S(1)}, u32[]{:S(2)}, u32[]{:S(2)}) collective-permute-start(f32[64,1,1024]{0,2,1:T(8,128)S(1)} %bitcast.269), channel_id=1, source_target_pairs={{4,0},{8,4},{12,8},{16,12},{20,16},{24,20},{28,24},{5,1},{9,5},{13... | collective-permute-start | bytes 786440 | tf_op jit(solution)/shard_map/ppermute | solution.py:20
  249.7 3.2 copy-start.2
  306.0 9.7 %collective-permute-start.4 = (f32[64,1,1024]{0,2,1:T(8,128)S(1)}, f32[64,1,1024]{0,2,1:T(8,128)S(1)}, u32[]{:S(2)}, u32[]{:S(2)}) collective-permute-start(f32[64,1,1024]{0,2,1:T(8,128)S(1)} %bitcast.275), channel_id=1, source_target_pairs={{0,4},{4,8},{8,12},{12,16},{16,20},{20,24},{24,28},{1,5},{5,9},{9,... | collective-permute-start | bytes 786440 | tf_op jit(solution)/shard_map/ppermute | solution.py:19
  307.9 18.7 %collective-permute-start.5 = (f32[64,1,1024]{0,2,1:T(8,128)S(1)}, f32[64,1,1024]{0,2,1:T(8,128)S(1)}, u32[]{:S(2)}, u32[]{:S(2)}) collective-permute-start(f32[64,1,1024]{0,2,1:T(8,128)S(1)} %bitcast.270), channel_id=1, source_target_pairs={{4,0},{8,4},{12,8},{16,12},{20,16},{24,20},{28,24},{5,1},{9,5},{13... | collective-permute-start | bytes 786440 | tf_op jit(solution)/shard_map/ppermute | solution.py:20
  398.7 9.9 %collective-permute-start.6 = (f32[64,1,1024]{0,2,1:T(8,128)S(1)}, f32[64,1,1024]{0,2,1:T(8,128)S(1)}, u32[]{:S(2)}, u32[]{:S(2)}) collective-permute-start(f32[64,1,1024]{0,2,1:T(8,128)S(1)} %bitcast.274), channel_id=1, source_target_pairs={{0,4},{4,8},{8,12},{12,16},{16,20},{20,24},{24,28},{1,5},{5,9},{9,... | collective-permute-start | bytes 786440 | tf_op jit(solution)/shard_map/ppermute | solution.py:19
  401.4 27.7 %collective-permute-start.7 = (f32[64,1,1024]{0,2,1:T(8,128)S(1)}, f32[64,1,1024]{0,2,1:T(8,128)S(1)}, u32[]{:S(2)}, u32[]{:S(2)}) collective-permute-start(f32[64,1,1024]{0,2,1:T(8,128)S(1)} %bitcast.271), channel_id=1, source_target_pairs={{4,0},{8,4},{12,8},{16,12},{20,16},{24,20},{28,24},{5,1},{9,5},{13... | collective-permute-start | bytes 786440 | tf_op jit(solution)/shard_map/ppermute | solution.py:20
  449.6 29.9 %all-to-all-start = ((bf16[64,4,3072]{2,0,1:T(8,128)(2,1)}), bf16[64,4,3072]{2,0,1:T(8,128)(2,1)S(1)}, u32[]{:S(2)}, u32[]{:S(2)}) async-start(bf16[64,4,3072]{2,0,1:T(8,128)(2,1)} %copy.74), calls=%async_computation | async-start | bytes 3145728 | tf_op jit(solution)/shard_map/all_to_all | solution.py:131
  454.4 177.9 %all-reduce.2.cloned.1.call-start = ((), (), s32[]{:S(2)}) async-start(), calls=%async_computation.2 | async-start | bytes 524288 | tf_op jit(solution)/shard_map/psum | solution.py:140
  641.4 40.2 %copy-start.1 = (bf16[512,512]{1,0:T(8,128)(2,1)S(1)}, bf16[512,512]{1,0:T(8,128)(2,1)}, u32[]{:S(2)}) copy-start(bf16[512,512]{1,0:T(8,128)(2,1)} %param.24) | copy-start | bytes 1572868
Sparse Core Ops, SparseCore 0:
  481.1 151.1 all-reduce.1
where the time goes:
time: 700 us; the launch traced here: 689 us
  local copies, waits for them, and re-layouts  188 us (27%)
  waiting for transfers between devices  174 us (25%)
  other arithmetic  155 us (22%)
  matrix products  71.8 us (10%)
  starting transfers between devices  46.2 us (7%)
  blocking collectives  37.9 us (5%)
  between operations  15.7 us (2%)
    psum x1, waiting for transfers between devices, body(): gram_matrix = lax.psum(partial_gram, ('dom', 'band'))  151 us
    scatter-add x8, other arithmetic, apply_field(): local_sum.at[:, left_face].add(padded[:, 0]).at[:, right_face]  87.2 us
    unnamed x30, local copies, waits for them, and re-layouts  51.1 us
    all_to_all x1, blocking collectives, body(): lax.all_to_all(rotated, 'band', split_axis=0, concat_axis=1, tiled=True)  37.9 us
    slice x12, local copies, waits for them, and re-layouts, local_apply(): folded = folded.at[:, :, 0].add(jnp.roll(split_terms[:, :, 3], 1, axis=1))  33.9 us
    ppermute x4, starting transfers between devices, with_halo(): after = lax.ppermute(first, axis, down)  31.3 us
    dot_general x4, matrix products, window_terms(): jnp.einsum('scb,cba->sca', windows, window_ops, preferred_element_type=jn...  26.2 us
    gather x4, local copies, waits for them, and re-layouts, apply_field(): local_sum[:, right_face]  23.7 us
  transfers between devices with their start and end apart: 10, of which 3 were waited for; matrix products, arithmetic and copies ran while one was open for 9% of the time, Pallas kernels for 0%

commit v1 on v0

v1 whole, which is shorter than its diff:
```python
import functools

import jax
import jax.numpy as jnp
from jax import lax
from jax.experimental import pallas as pl
from jax.experimental.pallas import tpu as pltpu
from jax.sharding import PartitionSpec as P

CHEB = 4
NS_ITERS = 5
GROUP = 4
VMEM_LIMIT = 56 * 1024 * 1024


def params():
    return pltpu.CompilerParams(vmem_limit_bytes=VMEM_LIMIT)


def vmem():
    return pl.BlockSpec(memory_space=pltpu.VMEM)


def smem():
    return pl.BlockSpec(memory_space=pltpu.SMEM)


def operators_kernel(node_total, counts_ref, conn_ref, pot_ref, kinetic_ref, ops_ref, diag_ref, ext):
    group, _, width = conn_ref.shape
    step = 3 * width // 4
    first = pl.program_id(0) * group

    @pl.when(pl.program_id(0) == 0)
    def _():
        ext[...] = jnp.zeros_like(ext)

    for j in range(group):
        cell = first + j
        slots = conn_ref[j] - cell * step
        slots = jnp.where(slots < 0, slots + node_total, slots)
        hit = lax.broadcasted_iota(jnp.int32, (width, width), 0) == slots
        perm = jnp.where(hit, 1.0, 0.0).astype(jnp.bfloat16)
        rows = jnp.dot(perm, kinetic_ref[...], preferred_element_type=jnp.float32)
        ops_ref[j] = lax.dot_general(
            rows.astype(jnp.bfloat16), perm, (((1,), (1,)), ((), ())),
            preferred_element_type=jnp.float32,
        ).astype(jnp.bfloat16)
        alive = jnp.where(cell < counts_ref[0], 1.0, 0.0)
        column = jnp.sum(jnp.where(hit, pot_ref[j] * alive, 0.0), axis=1, keepdims=True)
        span = pl.ds(pl.multiple_of(cell * step, 128), width)
        ext[span, :] = ext[span, :] + column

    @pl.when(pl.program_id(0) == pl.num_programs(0) - 1)
    def _():
        tail = width - step
        diag_ref[...] = ext[:node_total]
        diag_ref[:tail] = ext[:tail] + ext[node_total:]


def operators(connectivity, cell_kinetic, cell_potential, cell_counts, node_total):
    cells, width = connectivity.shape
    tail = width // 4
    return pl.pallas_call(
        functools.partial(operators_kernel, node_total),
        grid=(cells // GROUP,),
        in_specs=[
            smem(),
            pl.BlockSpec((GROUP, 1, width), lambda g: (g, 0, 0)),
            pl.BlockSpec((GROUP, 1, width), lambda g: (g, 0, 0)),
            pl.BlockSpec((width, width), lambda g: (0, 0)),
        ],
        out_specs=[
            pl.BlockSpec((GROUP, width, width), lambda g: (g, 0, 0)),
            pl.BlockSpec((node_total, 1), lambda g: (0, 0)),
        ],
        out_shape=[
            jax.ShapeDtypeStruct((cells, width, width), jnp.bfloat16),
            jax.ShapeDtypeStruct((node_total, 1), jnp.float32),
        ],
        scratch_shapes=[pltpu.VMEM((node_total + tail, 1), jnp.float32)],
        compiler_params=params(),
        name="window_operators",
    )(cell_counts, connectivity[:, None], cell_potential[:, None], cell_kinetic)


CHUNK = 16


def add_faces(faces_ref, halo, total):
    shared = faces_ref.shape[1]
    for side in range(2):

        def visit(i, carry, side=side):
            base = i * CHUNK
            nodes = [faces_ref[side, base + j] for j in range(CHUNK)]
            rows = [total[pl.ds(nodes[j], 1), :] for j in range(CHUNK)]
            gains = halo[pl.ds(pl.multiple_of(side * shared + base, CHUNK), CHUNK), :]
            for j in range(CHUNK):
                total[pl.ds(nodes[j], 1), :] = rows[j] + gains[j : j + 1]
            return carry

        lax.fori_loop(0, shared // CHUNK, visit, 0)


def pick_faces(faces_ref, total, halo):
    shared = faces_ref.shape[1]
    for side in range(2):

        def visit(i, carry, side=side):
            base = i * CHUNK
            nodes = [faces_ref[side, base + j] for j in range(CHUNK)]
            rows = [total[pl.ds(nodes[j], 1), :] for j in range(CHUNK)]
            halo[pl.ds(pl.multiple_of(side * shared + base, CHUNK), CHUNK), :] = jnp.concatenate(
                rows, axis=0
            )
            return carry

        lax.fori_loop(0, shared // CHUNK, visit, 0)


def unpack_halo(packed_refs, halo):
    for side, packed in enumerate(packed_refs):
        half, lanes = packed.shape
        base = side * 2 * half
        halo[base : base + half] = packed[:, : lanes // 2]
        halo[base + half : base + 2 * half] = packed[:, lanes // 2 :]


def pack_halo(halo, packed_refs):
    for side, packed in enumerate(packed_refs):
        half = packed.shape[0]
        base = side * 2 * half
        packed[...] = jnp.concatenate(
            [halo[base : base + half], halo[base + half : base + 2 * half]], axis=1
        )


ROWS = 768


def by_rows(total, visit):
    def step(i, carry):
        visit(pl.ds(pl.multiple_of(i * ROWS, ROWS), ROWS))
        return carry

    lax.fori_loop(0, total // ROWS, step, 0)


def apply_cells(counts_ref, scale_ref, ops_ref, field, ext):
    group, width, _ = ops_ref.shape
    step = 3 * width // 4
    for j in range(group):
        cell = pl.program_id(0) * group + j
        span = pl.ds(pl.multiple_of(cell * step, 128), width)
        scale = jnp.where(cell < counts_ref[0], scale_ref[cell], 0.0)
        product = jnp.dot(ops_ref[j], field[span, :], preferred_element_type=jnp.float32)
        ext[span, :] = ext[span, :] + product * scale


def apply_tail(faces_ref, local_ref, left_ref, right_ref, ext, halo):
    nodes = local_ref.shape[0]
    tail = ext.shape[0] - nodes
    ext[:tail] = ext[:tail] + ext[nodes:]
    pick_faces(faces_ref, ext, halo)
    pack_halo(halo, (left_ref, right_ref))

    def emit(rows):
        local_ref[rows, :] = ext[rows, :]

    by_rows(nodes, emit)


def first_kernel(counts_ref, scale_ref, faces_ref, ops_ref, diag_ref, states_ref,
                 local_ref, left_ref, right_ref, field, ext, halo):
    nodes = local_ref.shape[0]
    tail = ext.shape[0] - nodes

    @pl.when(pl.program_id(0) == 0)
    def _():
        def load(rows):
            value = states_ref[rows, :]
            field[rows, :] = value
            ext[rows, :] = value.astype(jnp.float32) * diag_ref[rows, :]

        by_rows(nodes, load)
        field[nodes:] = field[:tail]
        ext[nodes:] = jnp.zeros((tail, ext.shape[1]), jnp.float32)

    apply_cells(counts_ref, scale_ref, ops_ref, field, ext)

    @pl.when(pl.program_id(0) == pl.num_programs(0) - 1)
    def _():
        apply_tail(faces_ref, local_ref, left_ref, right_ref, ext, halo)


def next_kernel(twice, counts_ref, scale_ref, faces_ref, ops_ref, diag_ref, prev_ref, old_ref,
                from_left, from_right,
                local_ref, left_ref, right_ref, field_ref, field, ext, halo):
    nodes = local_ref.shape[0]
    tail = ext.shape[0] - nodes

    @pl.when(pl.program_id(0) == 0)
    def _():
        def load(rows):
            ext[rows, :] = old_ref[rows, :]

        by_rows(nodes, load)
        unpack_halo((from_left, from_right), halo)
        add_faces(faces_ref, halo, ext)

        def combine(rows):
            value = ext[rows, :]
            if twice:
                value = 2.0 * value - prev_ref[rows, :].astype(jnp.float32)
            value = value.astype(jnp.bfloat16)
            field[rows, :] = value
            field_ref[rows, :] = value
            ext[rows, :] = value.astype(jnp.float32) * diag_ref[rows, :]

        by_rows(nodes, combine)
        field[nodes:] = field[:tail]
        ext[nodes:] = jnp.zeros((tail, ext.shape[1]), jnp.float32)

    apply_cells(counts_ref, scale_ref, ops_ref, field, ext)

    @pl.when(pl.program_id(0) == pl.num_programs(0) - 1)
    def _():
        apply_tail(faces_ref, local_ref, left_ref, right_ref, ext, halo)


def last_kernel(faces_ref, prev_ref, old_ref, from_left, from_right, field_ref, ext, halo):
    nodes = old_ref.shape[0]

    def load(rows):
        ext[rows, :] = old_ref[rows, :]

    by_rows(nodes, load)
    unpack_halo((from_left, from_right), halo)
    add_faces(faces_ref, halo, ext)

    def combine(i, carry):
        rows = pl.ds(pl.multiple_of(i * 128, 128), 128)
        value = 2.0 * ext[rows, :] - prev_ref[rows, :].astype(jnp.float32)
        field_ref[:, rows] = value.T.astype(jnp.bfloat16)
        return carry

    lax.fori_loop(0, nodes // 128, combine, 0)


def newton(gram_matrix):
    identity = jnp.eye(gram_matrix.shape[0], dtype=jnp.float32)
    frobenius = jnp.sqrt(jnp.sum(gram_matrix * gram_matrix))
    scaled = gram_matrix / frobenius
    inverse_root = identity
    for repeat in range(NS_ITERS):
        factor = 1.5 * identity - 0.5 * jnp.dot(
            inverse_root, scaled, precision=lax.Precision.HIGHEST
        )
        scaled = jnp.dot(scaled, factor, precision=lax.Precision.HIGHEST)
        inverse_root = jnp.dot(factor, inverse_root, precision=lax.Precision.HIGHEST)
    return inverse_root.astype(jnp.bfloat16)


def newton_kernel(gram_ref, mixing_ref):
    mixing_ref[...] = newton(gram_ref[...])


def newton_call(gram_matrix):
    return pl.pallas_call(
        newton_kernel,
        in_specs=[vmem()],
        out_specs=vmem(),
        out_shape=jax.ShapeDtypeStruct(gram_matrix.shape, jnp.bfloat16),
        compiler_params=params(),
        name="newton",
    )(gram_matrix)


def body(states, cell_kinetic, cell_scale, cell_potential, connectivity, shared_nodes, cell_counts):
    domain = lax.axis_index("dom")
    domains = lax.axis_size("dom")
    state_rows, node_total = states.shape
    cells, width = connectivity.shape
    faces = shared_nodes[0]
    shared = faces.shape[1]
    tail = width // 4
    ops, diag = operators(connectivity, cell_kinetic, cell_potential, cell_counts, node_total)

    up = [(i, i + 1) for i in range(domains - 1)]
    down = [(i + 1, i) for i in range(domains - 1)]
    field_shape = jax.ShapeDtypeStruct((node_total, state_rows), jnp.bfloat16)
    outs = [
        jax.ShapeDtypeStruct((node_total, state_rows), jnp.float32),
        jax.ShapeDtypeStruct((shared // 2, 2 * state_rows), jnp.float32),
        jax.ShapeDtypeStruct((shared // 2, 2 * state_rows), jnp.float32),
    ]
    scratch = [
        pltpu.VMEM((node_total + tail, state_rows), jnp.bfloat16),
        pltpu.VMEM((node_total + tail, state_rows), jnp.float32),
        pltpu.VMEM((2 * shared, state_rows), jnp.float32),
    ]
    ops_spec = pl.BlockSpec((GROUP, width, width), lambda g: (g, 0, 0))

    def exchange(left, right):
        return (lax.ppermute(right, "dom", up), lax.ppermute(left, "dom", down))

    local, left, right = pl.pallas_call(
        first_kernel,
        grid=(cells // GROUP,),
        in_specs=[smem(), smem(), smem(), ops_spec, vmem(), vmem()],
        out_specs=[vmem()] * 3,
        out_shape=outs,
        scratch_shapes=scratch,
        compiler_params=params(),
        name="apply_first",
    )(cell_counts, cell_scale, faces, ops, diag, states.T)
    previous = states.T
    current = None
    for k in range(1, CHEB):
        halo = exchange(left, right)
        local, left, right, field = pl.pallas_call(
            functools.partial(next_kernel, k > 1),
            grid=(cells // GROUP,),
            in_specs=[smem(), smem(), smem(), ops_spec] + [vmem()] * 5,
            out_specs=[vmem()] * 4,
            out_shape=outs + [field_shape],
            scratch_shapes=scratch,
            compiler_params=params(),
            name="apply_next",
        )(cell_counts, cell_scale, faces, ops, diag, previous, local, *halo)
        if k > 1:
            previous = current
        current = field
    halo = exchange(left, right)
    filtered = pl.pallas_call(
        last_kernel,
        in_specs=[smem()] + [vmem()] * 4,
        out_specs=vmem(),
        out_shape=jax.ShapeDtypeStruct((state_rows, node_total), jnp.bfloat16),
        scratch_shapes=[
            pltpu.VMEM((node_total, state_rows), jnp.float32),
            pltpu.VMEM((2 * shared, state_rows), jnp.float32),
        ],
        compiler_params=params(),
        name="finish",
    )(faces, previous, local, *halo)

    row_shard = lax.all_to_all(filtered, "band", split_axis=1, concat_axis=0, tiled=True)
    piece_nodes = row_shard.shape[1]
    nodes = lax.axis_index("band") * piece_nodes + jnp.arange(piece_nodes, dtype=jnp.int32)
    has_left = (domain > 0).astype(jnp.float32)
    has_right = (domain < domains - 1).astype(jnp.float32)
    on_left = jnp.sum((nodes[None, :] == faces[0][:, None]).astype(jnp.float32), axis=0)
    on_right = jnp.sum((nodes[None, :] == faces[1][:, None]).astype(jnp.float32), axis=0)
    weight = (1.0 / (1.0 + has_left * on_left + has_right * on_right)).astype(jnp.bfloat16)
    weighted = row_shard * weight[None]
    partial_gram = lax.dot_general(
        weighted, row_shard, (((1,), (1,)), ((), ())), preferred_element_type=jnp.float32
    )
    gram_matrix = lax.psum(partial_gram, ("dom", "band"))
    mixing = newton_call(gram_matrix)
    rotated = lax.dot_general(
        mixing, row_shard, (((0,), (0,)), ((), ())), preferred_element_type=jnp.float32
    ).astype(jnp.bfloat16)
    return lax.all_to_all(rotated, "band", split_axis=0, concat_axis=1, tiled=True)


def solution(mesh):
    in_specs = (
        P("band", "dom"),
        P(),
        P("dom"),
        P("dom", None),
        P("dom", None),
        P("dom", None, None),
        P("dom"),
    )
    out_specs = P("band", "dom")
    return jax.shard_map(body, mesh=mesh, in_specs=in_specs, out_specs=out_specs, check_vma=False)
```

time: 700 us -> 459 us (0.66)
  Pallas kernels: 0 us -> 179 us
  local copies, waits for them, and re-layouts: 188 us -> 14 us
  other arithmetic: 155 us -> 3 us
  matrix products: 71.8 us -> 2.81 us
  starting transfers between devices: 46.2 us -> 23.5 us
    pallas_call x0 -> x7, Pallas kernels: none -> 179 us  [the longest x3 102 us: body(): pl.pallas_call(functools.partial(next_kernel, k > 1), grid=(cells // GROU...]
    scatter-add x14 -> x0, other arithmetic: 112 us -> none  [the longest x8 87.2 us: apply_field(): local_sum.at[:, left_face].add(padded[:, 0]).at[:, right_face]]
    dot_general x20 -> x0, matrix products: 69.9 us -> none  [the longest x4 26.2 us: window_terms(): jnp.einsum('scb,cba->sca', windows, window_ops, preferred_element_type=jn...]
    gather x8 -> x0, local copies, waits for them, and re-layouts: 46.4 us -> none  [the longest x4 23.7 us: apply_field(): local_sum[:, right_face]]
    unnamed x30 -> x19, local copies, waits for them, and re-layouts: 51.1 us -> 6.98 us
    reshape x9 -> x0, local copies, waits for them, and re-layouts: 38.3 us -> none  [the longest x4 21.1 us: local_apply(): split_terms = terms.reshape(state_rows, cell_total, 4, quarter)]
    slice x21 -> x1, local copies, waits for them, and re-layouts: 35.3 us -> 0.01 us  [body(): faces[1][:, None]]
    psum x1, waiting for transfers between devices: 151 us -> 127 us  [body(): gram_matrix = lax.psum(partial_gram, ('dom', 'band'))]
  transfers between devices with their start and end apart: 10 -> 10, of which waited for: 3 -> 10; matrix products, arithmetic and copies ran while one was open for 9% -> 1% of each run, Pallas kernels for 0% -> 0%
where the time goes in v1:
time: 459 us; the launch traced here: 454 us
  Pallas kernels  179 us (39%)
  waiting for transfers between devices  179 us (39%)
  blocking collectives  37.9 us (8%)
  starting transfers between devices  23.5 us (5%)
  between operations  14.2 us (3%)
  local copies, waits for them, and re-layouts  14 us (3%)
    psum x1, waiting for transfers between devices, body(): gram_matrix = lax.psum(partial_gram, ('dom', 'band'))  127 us
    pallas_call x3, Pallas kernels, body(): pl.pallas_call(functools.partial(next_kernel, k > 1), grid=(cells // GROU...  102 us
    all_to_all x1, blocking collectives, body(): lax.all_to_all(rotated, 'band', split_axis=0, concat_axis=1, tiled=True)  37.9 us
    all_to_all x1, waiting for transfers between devices, body(): lax.all_to_all(filtered, 'band', split_axis=1, concat_axis=0, tiled=True)  27.7 us
    pallas_call x1, Pallas kernels, operators(): pl.pallas_call(functools.partial(operators_kernel, node_total), grid=(cel...  25.6 us
    ppermute x8, waiting for transfers between devices, exchange(): return (lax.ppermute(right, 'dom', up), lax.ppermute(left, 'dom', down))  25.1 us
    pallas_call x1, Pallas kernels, body(): pl.pallas_call(first_kernel, grid=(cells // GROUP,), in_specs=[smem(), sm...  24.5 us
    pallas_call x1, Pallas kernels, body(): pl.pallas_call(last_kernel, in_specs=[smem()] + [vmem()] * 4, out_specs=v...  19.9 us
  transfers between devices with their start and end apart: 10, of which 10 were waited for; matrix products, arithmetic and copies ran while one was open for 1% of the time, Pallas kernels for 0%

profile of v1, /device:TPU:9, one launch (start us, length us, event | category | flops | bytes accessed | tf_op | source)
XLA Modules:
  0.0 453.7 jit_solution(8326566860239982591)
XLA Ops:
  7.2 1.5 broadcast_in_dim.10.pot_ref
  8.7 1.5 broadcast_in_dim.4.conn_ref
  10.2 4.2 copy.13
  14.4 25.6 %window_operators.1 = (bf16[32,512,512]{2,1,0:T(8,128)(2,1)}, f32[12288,1]{1,0:T(8,128)}) custom-call(s32[1]{0:T(128)S(6)} %copy.21.counts_ref, s32[32,1,512]{2,1,0:T(1,128)} %broadcast_in_dim.4.conn_ref, f32[32,1,512]{2,1,0:T(1,128)} %broadcast_in_dim.10.pot_ref, bf16[512,512]{1,0:T(8,128)(2,1)} %kinetic_ref.1), custom_call_target="tpu_custom_call" | custom-call | tf_op jit(solution)/shard_map/window_operators/pallas_call | solution.py:63
  39.9 24.5 %apply_first.1 = (f32[12288,64]{1,0:T(8,128)}, f32[512,128]{1,0:T(8,128)}, f32[512,128]{1,0:T(8,128)}) custom-call(s32[1]{0:T(128)S(6)} %copy.21.counts_ref, f32[32]{0:T(128)} %scale_ref.7, s32[2,1024]{1,0:T(2,128)} %bitcast.30, bf16[32,512,512]{2,1,0:T(8,128)(2,1)} %get-tuple-element.21.ops_ref, f32[12288,1]{1,0:T(8,128)} %get-tuple-element.22.diag_ref, ...), custom_call_target="tpu_custom_call" | custom-call | tf_op jit(solution)/shard_map/apply_first/pallas_call | solution.py:307
  64.4 3.7 collective-permute-start
  68.1 1.9 collective-permute-start.1
  70.1 1.7 collective-permute-done.from_left
  71.7 0.0 copy-start.3
  71.7 4.3 collective-permute-done.1.from_right
  76.1 0.0 copy-done.3
  76.1 0.7 copy-done.5
  76.8 33.9 %apply_next.3 = (f32[12288,64]{1,0:T(8,128)}, f32[512,128]{1,0:T(8,128)}, f32[512,128]{1,0:T(8,128)}, bf16[12288,64]{1,0:T(8,128)(2,1)}) custom-call(s32[1]{0:T(128)S(6)} %copy.21.counts_ref, f32[32]{0:T(128)} %scale_ref.7, s32[2,1024]{1,0:T(2,128)} %bitcast.31, bf16[32,512,512]{2,1,0:T(8,128)(2,1)} %get-tuple-element.21.ops_ref, ...), custom_call_target="tpu_custom_call" | custom-call | tf_op jit(solution)/shard_map/apply_next/pallas_call | solution.py:321
  110.7 1.9 collective-permute-start.2
  112.6 2.4 collective-permute-start.3
  115.0 1.2 collective-permute-done.2.from_left
  116.2 5.2 %collective-permute-done.3.from_right = f32[512,128]{1,0:T(8,128)S(1)} collective-permute-done((f32[512,128]{1,0:T(8,128)}, f32[512,128]{1,0:T(8,128)S(1)}, u32[]{:S(2)}, u32[]{:S(2)}) %collective-permute-start.3) | collective-permute-done | bytes 262176 | tf_op jit(solution)/shard_map/ppermute | solution.py:305
  121.4 0.0 copy-done.4
  121.4 0.7 copy-done.6
  122.1 33.9 %apply_next.4 = (f32[12288,64]{1,0:T(8,128)}, f32[512,128]{1,0:T(8,128)}, f32[512,128]{1,0:T(8,128)}, bf16[12288,64]{1,0:T(8,128)(2,1)}) custom-call(s32[1]{0:T(128)S(6)} %copy.21.counts_ref, f32[32]{0:T(128)} %scale_ref.7, s32[2,1024]{1,0:T(2,128)} %bitcast.32, bf16[32,512,512]{2,1,0:T(8,128)(2,1)} %get-tuple-element.21.ops_ref, ...), custom_call_target="tpu_custom_call" | custom-call | tf_op jit(solution)/shard_map/apply_next/pallas_call | solution.py:321
  156.0 1.9 collective-permute-start.4
  157.9 2.4 collective-permute-start.5
  160.3 1.2 collective-permute-done.4.from_left
  161.5 5.2 %collective-permute-done.5.from_right = f32[512,128]{1,0:T(8,128)S(1)} collective-permute-done((f32[512,128]{1,0:T(8,128)}, f32[512,128]{1,0:T(8,128)S(1)}, u32[]{:S(2)}, u32[]{:S(2)}) %collective-permute-start.5) | collective-permute-done | bytes 262176 | tf_op jit(solution)/shard_map/ppermute | solution.py:305
  166.7 0.0 copy-done.1
  166.7 0.7 copy-done.2
  167.4 33.9 %apply_next.5 = (f32[12288,64]{1,0:T(8,128)}, f32[512,128]{1,0:T(8,128)}, f32[512,128]{1,0:T(8,128)}, bf16[12288,64]{1,0:T(8,128)(2,1)}) custom-call(s32[1]{0:T(128)S(6)} %copy.21.counts_ref, f32[32]{0:T(128)} %scale_ref.7, s32[2,1024]{1,0:T(2,128)} %bitcast.33, bf16[32,512,512]{2,1,0:T(8,128)(2,1)} %get-tuple-element.21.ops_ref, ...), custom_call_target="tpu_custom_call" | custom-call | tf_op jit(solution)/shard_map/apply_next/pallas_call | solution.py:321
  201.3 1.9 collective-permute-start.6
  203.2 2.4 collective-permute-start.7
  205.6 1.2 collective-permute-done.6.from_left
  206.8 5.2 %collective-permute-done.7.from_right = f32[512,128]{1,0:T(8,128)S(1)} collective-permute-done((f32[512,128]{1,0:T(8,128)}, f32[512,128]{1,0:T(8,128)S(1)}, u32[]{:S(2)}, u32[]{:S(2)}) %collective-permute-start.7) | collective-permute-done | bytes 262176 | tf_op jit(solution)/shard_map/ppermute | solution.py:305
  212.0 0.0 copy-done.7
  212.0 0.7 copy-done.8
  212.7 19.9 %finish.1 = bf16[64,12288]{1,0:T(8,128)(2,1)} custom-call(s32[2,1024]{1,0:T(2,128)} %bitcast.34, bf16[12288,64]{1,0:T(8,128)(2,1)} %get-tuple-element.29.prev_ref, f32[12288,64]{1,0:T(8,128)} %get-tuple-element.34.old_ref, f32[512,128]{1,0:T(8,128)} %copy-done.7, f32[512,128]{1,0:T(8,128)} %copy-done.8), custom_call_target="tpu_custom_call" | custom-call | tf_op jit(solution)/shard_map/finish/pallas_call | solution.py:335
  232.6 2.7 copy.19
  235.3 4.9 %all-to-all-start = ((bf16[64,4,3072]{2,0,1:T(8,128)(2,1)}), bf16[64,4,3072]{2,0,1:T(8,128)(2,1)S(1)}, u32[]{:S(2)}, u32[]{:S(2)}) async-start(bf16[64,4,3072]{2,0,1:T(8,128)(2,1)} %bitcast.20), calls=%async_computation | async-start | bytes 3145728 | tf_op jit(solution)/shard_map/all_to_all | solution.py:348
  240.2 0.0 all-reduce.2.cloned.1.call-start
  240.2 0.0 copy-done
  240.2 2.9 convert_reduce_fusion.1
  243.1 27.7 %all-to-all-done = bf16[64,4,3072]{2,0,1:T(8,128)(2,1)S(1)} async-done(((bf16[64,4,3072]{2,0,1:T(8,128)(2,1)}), bf16[64,4,3072]{2,0,1:T(8,128)(2,1)S(1)}, u32[]{:S(2)}, u32[]{:S(2)}) %all-to-all-start) | async-done | bytes 1572896 | tf_op jit(solution)/shard_map/all_to_all | solution.py:348
  270.8 0.1 bitcast_multiply_fusion
  270.9 1.3 fusion.1
  272.2 0.0 all-reduce.2.cloned.1.call-update
  272.3 126.7 %all-reduce.2.cloned.1.call-done.gram_ref = f32[256,256]{1,0:T(8,128)} async-done(((f32[256,256]{1,0:T(8,128)}), f32[256,256]{1,0:T(8,128)}) %all-reduce.2.cloned.1.call-update) | async-done | bytes 262160 | tf_op jit(solution)/shard_map/psum | solution.py:360
  399.0 7.2 %newton.1 = bf16[256,256]{1,0:T(8,128)(2,1)} custom-call(f32[256,256]{1,0:T(8,128)} %all-reduce.2.cloned.1.call-done.gram_ref), custom_call_target="tpu_custom_call" | custom-call | tf_op jit(solution)/shard_map/newton/pallas_call | solution.py:269
  406.2 1.5 convolution_convert_fusion
  407.7 37.9 %all_to_all.38 = bf16[4,64,3072]{2,1,0:T(8,128)(2,1)S(1)} all-to-all(bf16[4,64,3072]{2,1,0:T(8,128)(2,1)S(1)} %bitcast.27), channel_id=1, replica_groups=mesh['dom'=8,'band'=4] {'band'}, dimensions={0} | all-to-all | bytes 3145728 | tf_op jit(solution)/shard_map/all_to_all | solution.py:365
  445.6 1.3 copy.17
  (11 shorter events, 0.0 us)
Async XLA Ops:
  64.4 7.3 %collective-permute-start = (f32[512,128]{1,0:T(8,128)}, f32[512,128]{1,0:T(8,128)S(1)}, u32[]{:S(2)}, u32[]{:S(2)}) collective-permute-start(f32[512,128]{1,0:T(8,128)} %get-tuple-element.24), channel_id=1, source_target_pairs={{0,4},{4,8},{8,12},{12,16},{16,20},{20,24},{24,28},{1,5},{5,9},{9,... | collective-permute-start | bytes 786440 | tf_op jit(solution)/shard_map/ppermute | solution.py:305
  68.1 7.9 %collective-permute-start.1 = (f32[512,128]{1,0:T(8,128)}, f32[512,128]{1,0:T(8,128)S(1)}, u32[]{:S(2)}, u32[]{:S(2)}) collective-permute-start(f32[512,128]{1,0:T(8,128)} %get-tuple-element.25), channel_id=1, source_target_pairs={{4,0},{8,4},{12,8},{16,12},{20,16},{24,20},{28,24},{5,1},{9,5},{13... | collective-permute-start | bytes 786440 | tf_op jit(solution)/shard_map/ppermute | solution.py:305
  71.7 4.3 copy-start.3
  76.0 0.7 copy-start.5
  110.7 5.5 %collective-permute-start.2 = (f32[512,128]{1,0:T(8,128)}, f32[512,128]{1,0:T(8,128)S(1)}, u32[]{:S(2)}, u32[]{:S(2)}) collective-permute-start(f32[512,128]{1,0:T(8,128)} %get-tuple-element.27), channel_id=1, source_target_pairs={{0,4},{4,8},{8,12},{12,16},{16,20},{20,24},{24,28},{1,5},{5,9},{9,... | collective-permute-start | bytes 786440 | tf_op jit(solution)/shard_map/ppermute | solution.py:305
  112.6 8.8 %collective-permute-start.3 = (f32[512,128]{1,0:T(8,128)}, f32[512,128]{1,0:T(8,128)S(1)}, u32[]{:S(2)}, u32[]{:S(2)}) collective-permute-start(f32[512,128]{1,0:T(8,128)} %get-tuple-element.28), channel_id=1, source_target_pairs={{4,0},{8,4},{12,8},{16,12},{20,16},{24,20},{28,24},{5,1},{9,5},{13... | collective-permute-start | bytes 786440 | tf_op jit(solution)/shard_map/ppermute | solution.py:305
  116.2 5.2 %copy-start.4 = (f32[512,128]{1,0:T(8,128)}, f32[512,128]{1,0:T(8,128)S(1)}, u32[]{:S(2)}) copy-start(f32[512,128]{1,0:T(8,128)S(1)} %collective-permute-done.2.from_left) | copy-start | bytes 786436
  121.4 0.7 copy-start.6
  156.0 5.5 %collective-permute-start.4 = (f32[512,128]{1,0:T(8,128)}, f32[512,128]{1,0:T(8,128)S(1)}, u32[]{:S(2)}, u32[]{:S(2)}) collective-permute-start(f32[512,128]{1,0:T(8,128)} %get-tuple-element.32), channel_id=1, source_target_pairs={{0,4},{4,8},{8,12},{12,16},{16,20},{20,24},{24,28},{1,5},{5,9},{9,... | collective-permute-start | bytes 786440 | tf_op jit(solution)/shard_map/ppermute | solution.py:305
  157.9 8.8 %collective-permute-start.5 = (f32[512,128]{1,0:T(8,128)}, f32[512,128]{1,0:T(8,128)S(1)}, u32[]{:S(2)}, u32[]{:S(2)}) collective-permute-start(f32[512,128]{1,0:T(8,128)} %get-tuple-element.33), channel_id=1, source_target_pairs={{4,0},{8,4},{12,8},{16,12},{20,16},{24,20},{28,24},{5,1},{9,5},{13... | collective-permute-start | bytes 786440 | tf_op jit(solution)/shard_map/ppermute | solution.py:305
  161.5 5.2 %copy-start.1 = (f32[512,128]{1,0:T(8,128)}, f32[512,128]{1,0:T(8,128)S(1)}, u32[]{:S(2)}) copy-start(f32[512,128]{1,0:T(8,128)S(1)} %collective-permute-done.4.from_left) | copy-start | bytes 786436
  166.7 0.7 copy-start.2
  201.3 5.5 %collective-permute-start.6 = (f32[512,128]{1,0:T(8,128)}, f32[512,128]{1,0:T(8,128)S(1)}, u32[]{:S(2)}, u32[]{:S(2)}) collective-permute-start(f32[512,128]{1,0:T(8,128)} %get-tuple-element.35), channel_id=1, source_target_pairs={{0,4},{4,8},{8,12},{12,16},{16,20},{20,24},{24,28},{1,5},{5,9},{9,... | collective-permute-start | bytes 786440 | tf_op jit(solution)/shard_map/ppermute | solution.py:305
  203.2 8.8 %collective-permute-start.7 = (f32[512,128]{1,0:T(8,128)}, f32[512,128]{1,0:T(8,128)S(1)}, u32[]{:S(2)}, u32[]{:S(2)}) collective-permute-start(f32[512,128]{1,0:T(8,128)} %get-tuple-element.36), channel_id=1, source_target_pairs={{4,0},{8,4},{12,8},{16,12},{20,16},{24,20},{28,24},{5,1},{9,5},{13... | collective-permute-start | bytes 786440 | tf_op jit(solution)/shard_map/ppermute | solution.py:305
  206.8 5.2 %copy-start.7 = (f32[512,128]{1,0:T(8,128)}, f32[512,128]{1,0:T(8,128)S(1)}, u32[]{:S(2)}) copy-start(f32[512,128]{1,0:T(8,128)S(1)} %collective-permute-done.6.from_left) | copy-start | bytes 786436
  212.0 0.7 copy-start.8
  235.3 4.9 %copy-start = (s32[1,2,1024]{2,1,0:T(2,128)S(1)}, s32[1,2,1024]{2,1,0:T(2,128)}, u32[]{:S(2)}) copy-start(s32[1,2,1024]{2,1,0:T(2,128)} %param.12) | copy-start | bytes 24580
  235.3 35.5 %all-to-all-start = ((bf16[64,4,3072]{2,0,1:T(8,128)(2,1)}), bf16[64,4,3072]{2,0,1:T(8,128)(2,1)S(1)}, u32[]{:S(2)}, u32[]{:S(2)}) async-start(bf16[64,4,3072]{2,0,1:T(8,128)(2,1)} %bitcast.20), calls=%async_computation | async-start | bytes 3145728 | tf_op jit(solution)/shard_map/all_to_all | solution.py:348
  240.2 158.8 %all-reduce.2.cloned.1.call-start = ((), (), s32[]{:S(2)}) async-start(), calls=%async_computation.2 | async-start | bytes 524288 | tf_op jit(solution)/shard_map/psum | solution.py:360
Sparse Core Ops, SparseCore 0:
  272.4 126.5 all-reduce.1

commit v2 on v1

v2 whole, which is shorter than its diff:
```python
import functools

import jax
import jax.numpy as jnp
from jax import lax
from jax.experimental import pallas as pl
from jax.experimental.pallas import tpu as pltpu
from jax.sharding import PartitionSpec as P

CHEB = 4
NS_ITERS = 5
GROUP = 4
VMEM_LIMIT = 56 * 1024 * 1024


def params():
    return pltpu.CompilerParams(vmem_limit_bytes=VMEM_LIMIT)


def vmem():
    return pl.BlockSpec(memory_space=pltpu.VMEM)


def smem():
    return pl.BlockSpec(memory_space=pltpu.SMEM)


def operators_kernel(node_total, counts_ref, conn_ref, pot_ref, kinetic_ref, ops_ref, diag_ref, ext):
    group, _, width = conn_ref.shape
    step = 3 * width // 4
    first = pl.program_id(0) * group

    @pl.when(pl.program_id(0) == 0)
    def _():
        ext[...] = jnp.zeros_like(ext)

    for j in range(group):
        cell = first + j
        slots = conn_ref[j] - cell * step
        slots = jnp.where(slots < 0, slots + node_total, slots)
        hit = lax.broadcasted_iota(jnp.int32, (width, width), 0) == slots
        perm = jnp.where(hit, 1.0, 0.0).astype(jnp.bfloat16)
        rows = jnp.dot(perm, kinetic_ref[...], preferred_element_type=jnp.float32)
        ops_ref[j] = lax.dot_general(
            rows.astype(jnp.bfloat16), perm, (((1,), (1,)), ((), ())),
            preferred_element_type=jnp.float32,
        ).astype(jnp.bfloat16)
        alive = jnp.where(cell < counts_ref[0], 1.0, 0.0)
        column = jnp.sum(jnp.where(hit, pot_ref[j] * alive, 0.0), axis=1, keepdims=True)
        span = pl.ds(pl.multiple_of(cell * step, 128), width)
        ext[span, :] = ext[span, :] + column

    @pl.when(pl.program_id(0) == pl.num_programs(0) - 1)
    def _():
        tail = width - step
        half, lanes = diag_ref.shape
        ext[:tail] = ext[:tail] + ext[node_total:]
        low = lax.broadcasted_iota(jnp.int32, (ROWS, lanes), 1) < lanes // 2
        for i in range(half // ROWS):
            diag_ref[i * ROWS : (i + 1) * ROWS] = jnp.where(
                low, ext[i * ROWS : (i + 1) * ROWS], ext[half + i * ROWS : half + (i + 1) * ROWS]
            )


def operators(connectivity, cell_kinetic, cell_potential, cell_counts, node_total, state_rows):
    cells, width = connectivity.shape
    tail = width // 4
    return pl.pallas_call(
        functools.partial(operators_kernel, node_total),
        grid=(cells // GROUP,),
        in_specs=[
            smem(),
            pl.BlockSpec((GROUP, 1, width), lambda g: (g, 0, 0)),
            pl.BlockSpec((GROUP, 1, width), lambda g: (g, 0, 0)),
            pl.BlockSpec((width, width), lambda g: (0, 0)),
        ],
        out_specs=[
            pl.BlockSpec((GROUP, width, width), lambda g: (g, 0, 0)),
            pl.BlockSpec((node_total // 2, 2 * state_rows), lambda g: (0, 0)),
        ],
        out_shape=[
            jax.ShapeDtypeStruct((cells, width, width), jnp.bfloat16),
            jax.ShapeDtypeStruct((node_total // 2, 2 * state_rows), jnp.float32),
        ],
        scratch_shapes=[pltpu.VMEM((node_total + tail, 1), jnp.float32)],
        compiler_params=params(),
        name="window_operators",
    )(cell_counts, connectivity[:, None], cell_potential[:, None], cell_kinetic)


CHUNK = 16


ROWS = 768


def by_rows(total, visit):
    def step(i, carry):
        visit(pl.multiple_of(i * ROWS, ROWS))
        return carry

    lax.fori_loop(0, total // ROWS, step, 0)


def swap_halves(value):
    lanes = value.shape[1]
    return jnp.concatenate([value[:, lanes // 2 :], value[:, : lanes // 2]], axis=1)


def add_faces(sides_ref, faces_ref, from_refs, halo, total):
    shared = faces_ref.shape[1]
    for side, packed in enumerate(from_refs):
        half, lanes = packed.shape
        base = side * shared
        rows = jnp.where(sides_ref[side] > 0, packed[...].astype(jnp.float32), 0.0)
        halo[base : base + half] = rows[:, : lanes // 2]
        halo[base + half : base + shared] = rows[:, lanes // 2 :]
    for side in range(2):

        def visit(i, carry, side=side):
            base = i * CHUNK
            nodes = [faces_ref[side, base + j] for j in range(CHUNK)]
            gains = [halo[pl.ds(side * shared + base + j, 1), :] for j in range(CHUNK)]
            rows = [total[pl.ds(nodes[j], 1), :] + gains[j] for j in range(CHUNK)]
            for j in range(CHUNK):
                total[pl.ds(nodes[j], 1), :] = rows[j]
            return carry

        lax.fori_loop(0, shared // CHUNK, visit, 0)


def pick_faces(faces_ref, nodes_ref, ext, half_nodes, picked, to_refs):
    shared = faces_ref.shape[1]
    half = shared // 2
    for side in range(2):

        def visit(i, carry, side=side):
            base = i * CHUNK
            nodes = [faces_ref[side, base + j] for j in range(CHUNK)]
            spots = [jnp.where(n >= half_nodes, n - half_nodes, n) for n in nodes]
            rows = [ext[pl.ds(spot, 1), :] for spot in spots]
            for j in range(CHUNK):
                picked[pl.ds(side * shared + base + j, 1), :] = rows[j]
            return carry

        lax.fori_loop(0, shared // CHUNK, visit, 0)
        base = side * shared
        lanes = picked.shape[1]
        low = lax.broadcasted_iota(jnp.int32, (half, lanes), 1) < lanes // 2
        first, second = picked[base : base + half], picked[base + half : base + shared]
        upper_first = nodes_ref[base : base + half] >= half_nodes
        upper_second = nodes_ref[base + half : base + shared] >= half_nodes
        first = jnp.where(upper_first, swap_halves(first), first)
        second = jnp.where(upper_second, second, swap_halves(second))
        to_refs[side][...] = jnp.where(low, first, second).astype(to_refs[side].dtype)


def apply_cells(counts_ref, scale_ref, low_ops, high_ops, field, ext):
    group, width, _ = low_ops.shape
    step = 3 * width // 4
    lanes = ext.shape[1]
    low = lax.broadcasted_iota(jnp.int32, (1, lanes), 1) < lanes // 2
    for j in range(group):
        cell = pl.program_id(0) * group + j
        upper = cell + pl.num_programs(0) * group
        span = pl.ds(pl.multiple_of(cell * step, 128), width)
        scale = jnp.where(cell < counts_ref[0], scale_ref[cell], 0.0)
        upper_scale = jnp.where(upper < counts_ref[0], scale_ref[upper], 0.0)
        window = field[span, :]
        first = jnp.dot(low_ops[j], window, preferred_element_type=jnp.float32)
        second = jnp.dot(high_ops[j], window, preferred_element_type=jnp.float32)
        ext[span, :] = ext[span, :] + jnp.where(low, first * scale, second * upper_scale)


def finish_cells(faces_ref, nodes_ref, local_ref, left_ref, right_ref, ext, picked):
    half = local_ref.shape[0]
    tail = ext.shape[0] - half
    ext[:tail] = ext[:tail] + swap_halves(ext[half:])
    pick_faces(faces_ref, nodes_ref, ext, half, picked, (left_ref, right_ref))

    def emit(base):
        local_ref[pl.ds(base, ROWS), :] = ext[pl.ds(base, ROWS), :]

    by_rows(half, emit)


def start_tail(field, ext, half):
    tail = ext.shape[0] - half
    field[half:] = swap_halves(field[:tail])
    ext[half:] = jnp.zeros((tail, ext.shape[1]), jnp.float32)


def first_kernel(counts_ref, scale_ref, faces_ref, nodes_ref, low_ops, high_ops, diag_ref,
                 states_ref, local_ref, left_ref, right_ref, field_ref, field, ext, picked):
    half = local_ref.shape[0]

    @pl.when(pl.program_id(0) == 0)
    def _():
        def load(i, carry):
            low = pl.ds(pl.multiple_of(i * 128, 128), 128)
            high = pl.ds(pl.multiple_of(half + i * 128, 128), 128)
            pair = jnp.concatenate([states_ref[:, low], states_ref[:, high]], axis=0)
            value = pair.astype(jnp.float32).T
            rounded = value.astype(jnp.bfloat16)
            field[low, :] = rounded
            field_ref[low, :] = rounded
            ext[low, :] = value * diag_ref[low, :]
            return carry

        lax.fori_loop(0, half // 128, load, 0)
        start_tail(field, ext, half)

    apply_cells(counts_ref, scale_ref, low_ops, high_ops, field, ext)

    @pl.when(pl.program_id(0) == pl.num_programs(0) - 1)
    def _():
        finish_cells(faces_ref, nodes_ref, local_ref, left_ref, right_ref, ext, picked)


def unpack_local(old_ref, total):
    half, lanes = old_ref.shape

    def load(base):
        value = old_ref[pl.ds(base, ROWS), :]
        total[pl.ds(base, ROWS), :] = value[:, : lanes // 2]
        total[pl.ds(half + base, ROWS), :] = value[:, lanes // 2 :]

    by_rows(half, load)


def next_kernel(twice, counts_ref, scale_ref, faces_ref, sides_ref, nodes_ref, low_ops, high_ops,
                diag_ref, prev_ref, old_ref, from_left, from_right,
                local_ref, left_ref, right_ref, field_ref, field, ext, picked, total, halo):
    half = local_ref.shape[0]

    @pl.when(pl.program_id(0) == 0)
    def _():
        unpack_local(old_ref, total)
        add_faces(sides_ref, faces_ref, (from_left, from_right), halo, total)

        def combine(base):
            rows = pl.ds(base, ROWS)
            value = jnp.concatenate([total[rows, :], total[pl.ds(half + base, ROWS), :]], axis=1)
            if twice:
                value = 2.0 * value - prev_ref[rows, :].astype(jnp.float32)
            value = value.astype(jnp.bfloat16)
            field[rows, :] = value
            field_ref[rows, :] = value
            ext[rows, :] = value.astype(jnp.float32) * diag_ref[rows, :]

        by_rows(half, combine)
        start_tail(field, ext, half)

    apply_cells(counts_ref, scale_ref, low_ops, high_ops, field, ext)

    @pl.when(pl.program_id(0) == pl.num_programs(0) - 1)
    def _():
        finish_cells(faces_ref, nodes_ref, local_ref, left_ref, right_ref, ext, picked)


def last_kernel(faces_ref, sides_ref, prev_ref, old_ref, from_left, from_right, field_ref,
                total, halo):
    half, lanes = old_ref.shape
    unpack_local(old_ref, total)
    add_faces(sides_ref, faces_ref, (from_left, from_right), halo, total)

    def combine(i, carry):
        low = pl.ds(pl.multiple_of(i * 128, 128), 128)
        high = pl.ds(pl.multiple_of(half + i * 128, 128), 128)
        value = jnp.concatenate([total[low, :], total[high, :]], axis=1)
        value = (2.0 * value - prev_ref[low, :].astype(jnp.float32)).T
        field_ref[:, low] = value[: lanes // 2].astype(jnp.bfloat16)
        field_ref[:, high] = value[lanes // 2 :].astype(jnp.bfloat16)
        return carry

    lax.fori_loop(0, half // 128, combine, 0)


def exchange_kernel(domains, left_ref, right_ref, from_left, from_right,
                    send_up, send_down, recv_up, recv_down):
    dom, band = lax.axis_index("dom"), lax.axis_index("band")
    barrier = pltpu.get_barrier_semaphore()
    has_left, has_right = dom > 0, dom < domains - 1

    @pl.when(has_left)
    def _():
        pl.semaphore_signal(barrier, inc=1, device_id=(dom - 1, band), device_id_type=MESH)

    @pl.when(has_right)
    def _():
        pl.semaphore_signal(barrier, inc=1, device_id=(dom + 1, band), device_id_type=MESH)

    pl.semaphore_wait(barrier, jnp.where(has_left & has_right, 2, 1))

    down = pltpu.make_async_remote_copy(
        src_ref=left_ref, dst_ref=from_right, send_sem=send_down, recv_sem=recv_down,
        device_id=(dom - 1, band), device_id_type=MESH)
    up = pltpu.make_async_remote_copy(
        src_ref=right_ref, dst_ref=from_left, send_sem=send_up, recv_sem=recv_up,
        device_id=(dom + 1, band), device_id_type=MESH)

    @pl.when(has_left)
    def _():
        down.start()

    @pl.when(has_right)
    def _():
        up.start()

    @pl.when(has_left)
    def _():
        down.wait_send()
        up.wait_recv()

    @pl.when(has_right)
    def _():
        up.wait_send()
        down.wait_recv()


def exchange(left, right):
    anywhere = pl.BlockSpec(memory_space=pl.ANY)
    return pl.pallas_call(
        functools.partial(exchange_kernel, lax.axis_size("dom")),
        in_specs=[anywhere] * 2,
        out_specs=[anywhere] * 2,
        out_shape=[jax.ShapeDtypeStruct(left.shape, left.dtype)] * 2,
        scratch_shapes=[pltpu.SemaphoreType.DMA] * 4,
        compiler_params=pltpu.CompilerParams(collective_id=1, has_side_effects=True),
        name="exchange",
    )(left, right)


def newton(gram_matrix):
    identity = jnp.eye(gram_matrix.shape[0], dtype=jnp.float32)
    frobenius = jnp.sqrt(jnp.sum(gram_matrix * gram_matrix))
    scaled = gram_matrix / frobenius
    inverse_root = identity
    for repeat in range(NS_ITERS):
        factor = 1.5 * identity - 0.5 * jnp.dot(
            inverse_root, scaled, precision=lax.Precision.HIGHEST
        )
        scaled = jnp.dot(scaled, factor, precision=lax.Precision.HIGHEST)
        inverse_root = jnp.dot(factor, inverse_root, precision=lax.Precision.HIGHEST)
    return inverse_root.astype(jnp.bfloat16)


MESH = pl.DeviceIdType.MESH


def gram_kernel(domains, bands, part_ref, mixing_ref, from_dom, from_band, total,
                send_dom, recv_dom, send_band, recv_band, send_back, recv_back):
    dom, band = lax.axis_index("dom"), lax.axis_index("band")
    rows = part_ref.shape[0] // domains

    def dom_peer(i):
        return (lax.rem(dom + i, domains), band)

    def band_peer(i):
        return (dom, lax.rem(band + i, bands))

    peers = [dom_peer(i) for i in range(1, domains)] + [band_peer(i) for i in range(1, bands)]
    barrier = pltpu.get_barrier_semaphore()
    for peer in peers:
        pl.semaphore_signal(barrier, inc=1, device_id=peer, device_id_type=MESH)
    pl.semaphore_wait(barrier, len(peers))

    def span(index):
        return pl.ds(pl.multiple_of(index * rows, 8), rows)

    scatter = []
    for i in range(1, domains):
        peer = dom_peer(i)
        scatter.append(pltpu.make_async_remote_copy(
            src_ref=part_ref.at[span(peer[0])], dst_ref=from_dom.at[i],
            send_sem=send_dom.at[i], recv_sem=recv_dom.at[i],
            device_id=peer, device_id_type=MESH))
    for copy in scatter:
        copy.start()
    own = part_ref[span(dom), :]
    for copy in scatter:
        copy.wait()
    for i in range(1, domains):
        own = own + from_dom[i]
    from_band[band] = own
    across = []
    for i in range(1, bands):
        across.append(pltpu.make_async_remote_copy(
            src_ref=from_band.at[band], dst_ref=from_band.at[band],
            send_sem=send_band.at[i], recv_sem=recv_band.at[i],
            device_id=band_peer(i), device_id_type=MESH))
    for copy in across:
        copy.start()
    for copy in across:
        copy.wait()
    summed = from_band[0]
    for i in range(1, bands):
        summed = summed + from_band[i]
    total[span(dom), :] = summed
    back = []
    for i in range(1, domains):
        back.append(pltpu.make_async_remote_copy(
            src_ref=total.at[span(dom)], dst_ref=total.at[span(dom)],
            send_sem=send_back.at[i], recv_sem=recv_back.at[i],
            device_id=dom_peer(i), device_id_type=MESH))
    for copy in back:
        copy.start()
    for copy in back:
        copy.wait()
    mixing_ref[...] = newton(total[...])


def gram_call(partial_gram):
    domains, bands = lax.axis_size("dom"), lax.axis_size("band")
    size = partial_gram.shape[0]
    rows = size // domains
    return pl.pallas_call(
        functools.partial(gram_kernel, domains, bands),
        in_specs=[vmem()],
        out_specs=vmem(),
        out_shape=jax.ShapeDtypeStruct((size, size), jnp.bfloat16),
        scratch_shapes=[
            pltpu.VMEM((domains, rows, size), jnp.float32),
            pltpu.VMEM((bands, rows, size), jnp.float32),
            pltpu.VMEM((size, size), jnp.float32),
            pltpu.SemaphoreType.DMA((domains,)),
            pltpu.SemaphoreType.DMA((domains,)),
            pltpu.SemaphoreType.DMA((bands,)),
            pltpu.SemaphoreType.DMA((bands,)),
            pltpu.SemaphoreType.DMA((domains,)),
            pltpu.SemaphoreType.DMA((domains,)),
        ],
        compiler_params=pltpu.CompilerParams(
            vmem_limit_bytes=VMEM_LIMIT, collective_id=0, has_side_effects=True
        ),
        name="gram_newton",
    )(partial_gram)


def body(states, cell_kinetic, cell_scale, cell_potential, connectivity, shared_nodes, cell_counts):
    domain = lax.axis_index("dom")
    domains = lax.axis_size("dom")
    state_rows, node_total = states.shape
    cells, width = connectivity.shape
    faces = shared_nodes[0]
    shared = faces.shape[1]
    tail = width // 4
    half = node_total // 2
    lanes = 2 * state_rows
    ops, diag = operators(
        connectivity, cell_kinetic, cell_potential, cell_counts, node_total, state_rows
    )
    sides = jnp.stack([domain > 0, domain < domains - 1]).astype(jnp.int32)
    face_nodes = faces.reshape(2 * shared, 1)

    field_shape = jax.ShapeDtypeStruct((half, lanes), jnp.bfloat16)
    outs = [
        jax.ShapeDtypeStruct((half, lanes), jnp.float32),
        jax.ShapeDtypeStruct((shared // 2, lanes), jnp.bfloat16),
        jax.ShapeDtypeStruct((shared // 2, lanes), jnp.bfloat16),
        field_shape,
    ]
    scratch = [
        pltpu.VMEM((half + tail, lanes), jnp.bfloat16),
        pltpu.VMEM((half + tail, lanes), jnp.float32),
        pltpu.VMEM((2 * shared, lanes), jnp.float32),
    ]
    total_scratch = [
        pltpu.VMEM((node_total, state_rows), jnp.float32),
        pltpu.VMEM((2 * shared, state_rows), jnp.float32),
    ]
    group = GROUP // 2
    steps = cells // GROUP
    ops_specs = [
        pl.BlockSpec((group, width, width), lambda g: (g, 0, 0)),
        pl.BlockSpec((group, width, width), lambda g: (g + steps, 0, 0)),
    ]
    local, left, right, previous = pl.pallas_call(
        first_kernel,
        grid=(steps,),
        in_specs=[smem()] * 3 + [vmem()] + ops_specs + [vmem()] * 2,
        out_specs=[vmem()] * 4,
        out_shape=outs,
        scratch_shapes=scratch,
        compiler_params=params(),
        name="apply_first",
    )(cell_counts, cell_scale, faces, face_nodes, ops, ops, diag, states)
    current = previous
    for k in range(1, CHEB):
        halo = exchange(left, right)
        local, left, right, field = pl.pallas_call(
            functools.partial(next_kernel, k > 1),
            grid=(steps,),
            in_specs=[smem()] * 4 + [vmem()] + ops_specs + [vmem()] * 5,
            out_specs=[vmem()] * 4,
            out_shape=outs,
            scratch_shapes=scratch + total_scratch,
            compiler_params=params(),
            name="apply_next",
        )(cell_counts, cell_scale, faces, sides, face_nodes, ops, ops, diag, previous, local, *halo)
        previous = current
        current = field
    halo = exchange(left, right)
    filtered = pl.pallas_call(
        last_kernel,
        in_specs=[smem()] * 2 + [vmem()] * 4,
        out_specs=vmem(),
        out_shape=jax.ShapeDtypeStruct((state_rows, node_total), jnp.bfloat16),
        scratch_shapes=total_scratch,
        compiler_params=params(),
        name="finish",
    )(faces, sides, previous, local, *halo)

    row_shard = lax.all_to_all(filtered, "band", split_axis=1, concat_axis=0, tiled=True)
    piece_nodes = row_shard.shape[1]
    nodes = lax.axis_index("band") * piece_nodes + jnp.arange(piece_nodes, dtype=jnp.int32)
    has_left = (domain > 0).astype(jnp.float32)
    has_right = (domain < domains - 1).astype(jnp.float32)
    on_left = jnp.sum((nodes[None, :] == faces[0][:, None]).astype(jnp.float32), axis=0)
    on_right = jnp.sum((nodes[None, :] == faces[1][:, None]).astype(jnp.float32), axis=0)
    weight = (1.0 / (1.0 + has_left * on_left + has_right * on_right)).astype(jnp.bfloat16)
    weighted = row_shard * weight[None]
    partial_gram = lax.dot_general(
        weighted, row_shard, (((1,), (1,)), ((), ())), preferred_element_type=jnp.float32
    )
    mixing = gram_call(partial_gram)
    rotated = lax.dot_general(
        mixing, row_shard, (((0,), (0,)), ((), ())), preferred_element_type=jnp.float32
    ).astype(jnp.bfloat16)
    return lax.all_to_all(rotated, "band", split_axis=0, concat_axis=1, tiled=True)


def solution(mesh):
    in_specs = (
        P("band", "dom"),
        P(),
        P("dom"),
        P("dom", None),
        P("dom", None),
        P("dom", None, None),
        P("dom"),
    )
    out_specs = P("band", "dom")
    return jax.shard_map(body, mesh=mesh, in_specs=in_specs, out_specs=out_specs, check_vma=False)
```

time: 459 us -> 310 us (0.68)
  waiting for transfers between devices: 179 us -> 29.2 us
  Pallas kernels: 179 us -> 216 us
  starting transfers between devices: 23.5 us -> 4.67 us
  between operations: 14.2 us -> 0.73 us
  local copies, waits for them, and re-layouts: 14 us -> 9.09 us
    psum x1 -> x0, waiting for transfers between devices: 127 us -> none  [body(): gram_matrix = lax.psum(partial_gram, ('dom', 'band'))]
    pallas_call x6 -> x10, Pallas kernels: 153 us -> 190 us  [the longest x3 94.3 us: body(): pl.pallas_call(functools.partial(next_kernel, k > 1), grid=(steps,), in_s...]
    ppermute x8 -> x0, waiting for transfers between devices: 25.1 us -> none  [exchange(): return (lax.ppermute(right, 'dom', up), lax.ppermute(left, 'dom', down))]
    ppermute x8 -> x0, starting transfers between devices: 18.6 us -> none  [exchange(): return (lax.ppermute(right, 'dom', up), lax.ppermute(left, 'dom', down))]
    unnamed x19 -> x4, local copies, waits for them, and re-layouts: 6.98 us -> 2.11 us
  transfers between devices with their start and end apart: 10 -> 1, of which waited for: 10 -> 1; matrix products, arithmetic and copies ran while one was open for 1% -> 1% of each run, Pallas kernels for 0% -> 0%
where the time goes in v2:
time: 310 us; the launch traced here: 305 us
  Pallas kernels  216 us (70%)
  blocking collectives  38.9 us (13%)
  waiting for transfers between devices  29.2 us (9%)
  local copies, waits for them, and re-layouts  9.09 us (3%)
  starting transfers between devices  4.67 us (2%)
  other arithmetic  3.66 us (1%)
    pallas_call x3, Pallas kernels, body(): pl.pallas_call(functools.partial(next_kernel, k > 1), grid=(steps,), in_s...  94.3 us
    all_to_all x1, blocking collectives, body(): lax.all_to_all(rotated, 'band', split_axis=0, concat_axis=1, tiled=True)  38.9 us
    all_to_all x1, waiting for transfers between devices, body(): lax.all_to_all(filtered, 'band', split_axis=1, concat_axis=0, tiled=True)  29.2 us
    pallas_call x1, Pallas kernels, body(): pl.pallas_call(first_kernel, grid=(steps,), in_specs=[smem()] * 3 + [vmem...  26.7 us
    pallas_call x1, Pallas kernels, gram_call(): pl.pallas_call(functools.partial(gram_kernel, domains, bands), in_specs=[...  26.4 us
    pallas_call x1, Pallas kernels, operators(): pl.pallas_call(functools.partial(operators_kernel, node_total), grid=(cel...  25.4 us
    pallas_call x4, Pallas kernels, exchange(): pl.pallas_call(functools.partial(exchange_kernel, lax.axis_size('dom')),...  23.7 us
    pallas_call x1, Pallas kernels, body(): pl.pallas_call(last_kernel, in_specs=[smem()] * 2 + [vmem()] * 4, out_spe...  19.4 us
  transfers between devices with their start and end apart: 1, of which 1 were waited for; matrix products, arithmetic and copies ran while one was open for 1% of the time, Pallas kernels for 0%

profile of v2, /device:TPU:9, one launch (start us, length us, event | category | flops | bytes accessed | tf_op | source)
XLA Modules:
  0.0 305.0 jit_solution(11035063027261447925)
XLA Ops:
  0.7 1.5 broadcast_in_dim.10.pot_ref
  2.2 1.5 broadcast_in_dim.4.conn_ref
  3.7 0.7 copy.23
  4.4 1.4 copy.24
  5.8 25.4 %window_operators.1 = (bf16[32,512,512]{2,1,0:T(8,128)(2,1)}, f32[6144,128]{1,0:T(8,128)}) custom-call(s32[1]{0:T(128)S(6)} %copy.27.counts_ref, s32[32,1,512]{2,1,0:T(1,128)} %broadcast_in_dim.4.conn_ref, f32[32,1,512]{2,1,0:T(1,128)} %broadcast_in_dim.10.pot_ref, bf16[512,512]{1,0:T(8,128)(2,1)} %kinetic_ref.1), custom_call_target="tpu_custom_call" | custom-call | tf_op jit(solution)/shard_map/window_operators/pallas_call | solution.py:68
  31.2 26.7 %apply_first.1 = (f32[6144,128]{1,0:T(8,128)}, bf16[512,128]{1,0:T(8,128)(2,1)}, bf16[512,128]{1,0:T(8,128)(2,1)}, bf16[6144,128]{1,0:T(8,128)(2,1)}) custom-call(s32[1]{0:T(128)S(6)} %copy.27.counts_ref, f32[32]{0:T(128)} %scale_ref.7, s32[2,1024]{1,0:T(2,128)} %bitcast.36, s32[2048,1]{1,0:T(8,128)} %bitcast.25, ...), custom_call_target="tpu_custom_call" | custom-call | tf_op jit(solution)/shard_map/apply_first/pallas_call | solution.py:478
  57.9 5.3 %exchange.4 = (bf16[512,128]{1,0:T(8,128)(2,1)}, bf16[512,128]{1,0:T(8,128)(2,1)}) custom-call(bf16[512,128]{1,0:T(8,128)(2,1)} %get-tuple-element.34.left_ref, bf16[512,128]{1,0:T(8,128)(2,1)} %get-tuple-element.35.right_ref), custom_call_target="tpu_custom_call" | custom-call | tf_op jit(solution)/shard_map/exchange/pallas_call | solution.py:323
  63.2 0.7 add_convert_fusion.sides_ref
  63.9 31.2 %apply_next.3 = (f32[6144,128]{1,0:T(8,128)}, bf16[512,128]{1,0:T(8,128)(2,1)}, bf16[512,128]{1,0:T(8,128)(2,1)}, bf16[6144,128]{1,0:T(8,128)(2,1)}) custom-call(s32[1]{0:T(128)S(6)} %copy.27.counts_ref, f32[32]{0:T(128)} %scale_ref.7, s32[2,1024]{1,0:T(2,128)} %bitcast.37, s32[2]{0:T(128)} %add_convert_fusion.sides_ref, s32[2048,1]{1,0:T(8,128)} %bitcast.26, ...), custom_call_target="tpu_custom_call" | custom-call | tf_op jit(solution)/shard_map/apply_next/pallas_call | solution.py:491
  95.1 7.5 %exchange.5 = (bf16[512,128]{1,0:T(8,128)(2,1)}, bf16[512,128]{1,0:T(8,128)(2,1)}) custom-call(bf16[512,128]{1,0:T(8,128)(2,1)} %get-tuple-element.39.left_ref, bf16[512,128]{1,0:T(8,128)(2,1)} %get-tuple-element.40.right_ref), custom_call_target="tpu_custom_call" | custom-call | tf_op jit(solution)/shard_map/exchange/pallas_call | solution.py:323
  102.6 31.5 %apply_next.4 = (f32[6144,128]{1,0:T(8,128)}, bf16[512,128]{1,0:T(8,128)(2,1)}, bf16[512,128]{1,0:T(8,128)(2,1)}, bf16[6144,128]{1,0:T(8,128)(2,1)}) custom-call(s32[1]{0:T(128)S(6)} %copy.27.counts_ref, f32[32]{0:T(128)} %scale_ref.7, s32[2,1024]{1,0:T(2,128)} %bitcast.38, s32[2]{0:T(128)} %add_convert_fusion.sides_ref, s32[2048,1]{1,0:T(8,128)} %bitcast.27, ...), custom_call_target="tpu_custom_call" | custom-call | tf_op jit(solution)/shard_map/apply_next/pallas_call | solution.py:491
  134.2 5.6 %exchange.6 = (bf16[512,128]{1,0:T(8,128)(2,1)}, bf16[512,128]{1,0:T(8,128)(2,1)}) custom-call(bf16[512,128]{1,0:T(8,128)(2,1)} %get-tuple-element.46.left_ref, bf16[512,128]{1,0:T(8,128)(2,1)} %get-tuple-element.47.right_ref), custom_call_target="tpu_custom_call" | custom-call | tf_op jit(solution)/shard_map/exchange/pallas_call | solution.py:323
  139.8 31.6 %apply_next.5 = (f32[6144,128]{1,0:T(8,128)}, bf16[512,128]{1,0:T(8,128)(2,1)}, bf16[512,128]{1,0:T(8,128)(2,1)}, bf16[6144,128]{1,0:T(8,128)(2,1)}) custom-call(s32[1]{0:T(128)S(6)} %copy.27.counts_ref, f32[32]{0:T(128)} %scale_ref.7, s32[2,1024]{1,0:T(2,128)} %bitcast.39, s32[2]{0:T(128)} %add_convert_fusion.sides_ref, s32[2048,1]{1,0:T(8,128)} %bitcast.28, ...), custom_call_target="tpu_custom_call" | custom-call | tf_op jit(solution)/shard_map/apply_next/pallas_call | solution.py:491
  171.3 5.3 %exchange.7 = (bf16[512,128]{1,0:T(8,128)(2,1)}, bf16[512,128]{1,0:T(8,128)(2,1)}) custom-call(bf16[512,128]{1,0:T(8,128)(2,1)} %get-tuple-element.51.left_ref, bf16[512,128]{1,0:T(8,128)(2,1)} %get-tuple-element.52.right_ref), custom_call_target="tpu_custom_call" | custom-call | tf_op jit(solution)/shard_map/exchange/pallas_call | solution.py:323
  176.6 19.4 %finish.1 = bf16[64,12288]{1,0:T(8,128)(2,1)} custom-call(s32[2,1024]{1,0:T(2,128)} %bitcast.40, s32[2]{0:T(128)} %add_convert_fusion.sides_ref, bf16[6144,128]{1,0:T(8,128)(2,1)} %get-tuple-element.43.prev_ref, f32[6144,128]{1,0:T(8,128)} %get-tuple-element.50.old_ref, bf16[512,128]{1,0:T(8,128)(2,1)} %get-tuple-element.53.from_left, ...), custom_call_target="tpu_custom_call" | custom-call | tf_op jit(solution)/shard_map/finish/pallas_call | solution.py:504
  196.0 2.7 copy.26
  198.7 0.0 copy-start
  198.7 4.7 %all-to-all-start = ((bf16[64,4,3072]{2,0,1:T(8,128)(2,1)}), bf16[64,4,3072]{2,0,1:T(8,128)(2,1)S(1)}, u32[]{:S(2)}, u32[]{:S(2)}) async-start(bf16[64,4,3072]{2,0,1:T(8,128)(2,1)} %bitcast.24), calls=%async_computation | async-start | bytes 3145728 | tf_op jit(solution)/shard_map/all_to_all | solution.py:514
  203.4 0.0 copy-done
  203.4 2.9 convert_reduce_fusion.1
  206.3 29.2 %all-to-all-done = bf16[64,4,3072]{2,0,1:T(8,128)(2,1)S(1)} async-done(((bf16[64,4,3072]{2,0,1:T(8,128)(2,1)}), bf16[64,4,3072]{2,0,1:T(8,128)(2,1)S(1)}, u32[]{:S(2)}, u32[]{:S(2)}) %all-to-all-start) | async-done | bytes 1572896 | tf_op jit(solution)/shard_map/all_to_all | solution.py:514
  235.5 0.1 bitcast_multiply_fusion
  235.6 1.3 fusion.1.part_ref
  236.9 26.4 %gram_newton.1 = bf16[256,256]{1,0:T(8,128)(2,1)} custom-call(f32[256,256]{1,0:T(8,128)} %fusion.1.part_ref), custom_call_target="tpu_custom_call" | custom-call | tf_op jit(solution)/shard_map/gram_newton/pallas_call | solution.py:417
  263.3 1.5 convolution_convert_fusion
  264.8 38.9 %all_to_all.38 = bf16[4,64,3072]{2,1,0:T(8,128)(2,1)S(1)} all-to-all(bf16[4,64,3072]{2,1,0:T(8,128)(2,1)S(1)} %bitcast.31), channel_id=1, replica_groups=mesh['dom'=8,'band'=4] {'band'}, dimensions={0} | all-to-all | bytes 3145728 | tf_op jit(solution)/shard_map/all_to_all | solution.py:530
  303.7 1.3 copy.22
  (3 shorter events, 0.0 us)
Async XLA Ops:
  198.7 4.7 %copy-start = (s32[1,2,1024]{2,1,0:T(2,128)S(1)}, s32[1,2,1024]{2,1,0:T(2,128)}, u32[]{:S(2)}) copy-start(s32[1,2,1024]{2,1,0:T(2,128)} %param.12) | copy-start | bytes 24580
  198.7 36.8 %all-to-all-start = ((bf16[64,4,3072]{2,0,1:T(8,128)(2,1)}), bf16[64,4,3072]{2,0,1:T(8,128)(2,1)S(1)}, u32[]{:S(2)}, u32[]{:S(2)}) async-start(bf16[64,4,3072]{2,0,1:T(8,128)(2,1)} %bitcast.24), calls=%async_computation | async-start | bytes 3145728 | tf_op jit(solution)/shard_map/all_to_all | solution.py:514
